TPU v7x, 1024 devices: a whole 4x8x16 slice. The times are simulated.
1024 devices in a mesh: dp: 256 (over z, y_lo, x), space: 4 (over y_hi, core).
Axes of the slice: x: 4, y: 8 (y_hi: 2, y_lo: 4; y = y_hi * 4 + y_lo), z: 16, core: 2. Of those that a mesh axis runs over, the one named last changes fastest.
Arguments:
- features: bfloat16 [256, 12, 48, 3072], P('dp', 'space'), may hold values from -6 to 6
- norm_grad: bfloat16 [256, 12, 48, 3072], P('dp', 'space'), may hold values from -24 to 24
- token_grads: bfloat16 [256, 620, 3072], P('dp', 'space'), may hold values from -6 to 6
- token_place: int32 [256, 12, 48], P('dp', 'space'), may hold values from 0 to 618, as said below
- valid_rows: int32 [256], P('dp'), may hold values from 6 to 12, as said below
- depth_kernel: bfloat16 [7, 7, 3072], replicated, may hold values from -0.875 to 0.875
- depth_bias: float32 [3072], replicated, may hold values from -4 to 4
- norm_gain: float32 [3072], replicated, may hold values from 0.1 to 1.9
Outputs:
- input_grads: bfloat16 [256, 12, 48, 3072], P('dp', 'space')
- param_grads: float32 [52, 3072], P(None, 'dp')
Inputs may be any that keep to these rules, and one draw needn't show every extreme that they name: For each image i there is a prefix p_i with 0 <= p_i <= 32 such that token_place[i, r, c] = p_i + r * 49 + c; some image has p_i = 32 and some has p_i = 0. `valid_rows`: some image has all 12 rows valid and some has 6.
All inputs are finite; a program needn't handle non-finite values.
Results may differ from a plain program's by a relative error of at most 0.004.
Values may be sent and summed in bfloat16 or wider, within the bound.
A program may use at most 64 MiB of HBM per device.

v0:
```python
import jax
import jax.numpy as jnp
from jax import lax
from jax.sharding import PartitionSpec as P

KERNEL = 7


def padded(block, sides, width):
    for axis, dim in sides:
        count = lax.axis_size(axis)
        forward = [(i, i + 1) for i in range(count - 1)]
        backward = [(target, source) for source, target in forward]
        low = lax.ppermute(
            lax.slice_in_dim(block, block.shape[dim] - width, None, axis=dim), axis, forward
        )
        high = lax.ppermute(lax.slice_in_dim(block, 0, width, axis=dim), axis, backward)
        block = jnp.concatenate([low, block, high], axis=dim)
    return block


def grouped_conv(lhs, rhs, col_pad):
    return lax.conv_general_dilated(
        lhs,
        rhs,
        (1, 1),
        ((0, 0), (col_pad, col_pad)),
        dimension_numbers=("NHWC", "HWIO", "NHWC"),
        feature_group_count=lhs.shape[-1],
        preferred_element_type=jnp.float32,
    )


def norm_backward(mixed, norm_piece, norm_gain):
    center = jnp.mean(mixed, axis=-1, keepdims=True)
    offset = mixed - center
    spread = jnp.mean(offset * offset, axis=-1, keepdims=True)
    inverse = lax.rsqrt(spread + 1e-06)
    normed = offset * inverse
    upstream = norm_piece.astype(jnp.float32)
    scaled = upstream * norm_gain
    grad_mixed = inverse * (
        scaled
        - jnp.mean(scaled, axis=-1, keepdims=True)
        - normed * jnp.mean(scaled * normed, axis=-1, keepdims=True)
    )
    return (grad_mixed.astype(jnp.bfloat16), normed, upstream)


def body(
    features, norm_grad, token_grads, token_place, valid_rows, depth_kernel, depth_bias, norm_gain
):
    margin = KERNEL // 2
    height, columns, channels = (features.shape[1], features.shape[2], features.shape[3])
    seq_block = token_grads.shape[1]
    space_index = lax.axis_index("space")
    extended = padded(features, (("space", 1),), margin)
    mixed = depth_bias + grouped_conv(extended, depth_kernel[:, :, None, :], margin)[0]
    grad_half, normed, upstream = norm_backward(mixed, norm_grad[0], norm_gain)
    grad_wide = padded(grad_half[None], (("space", 1),), margin)
    nearby = padded(token_grads, (("space", 1),), seq_block)
    local_place = token_place[0] - space_index * seq_block + seq_block
    picked = nearby[0][local_place.reshape(-1)].reshape(height, columns, -1).astype(jnp.float32)
    row_ids = space_index * height + jnp.arange(height, dtype=jnp.int32)
    live_rows = (row_ids < valid_rows[0])[:, None, None]
    residual = jnp.where(live_rows, picked, jnp.float32(0.0))
    flipped = depth_kernel[::-1, ::-1][:, :, None, :]
    input_grad = (residual + grouped_conv(grad_wide, flipped, margin)[0]).astype(jnp.bfloat16)
    padded_wide = jnp.pad(extended, ((0, 0), (0, 0), (margin, margin), (0, 0)))
    tap_grads = grouped_conv(padded_wide, grad_half[:, :, None, :], 0)[0].reshape(
        KERNEL * KERNEL, channels
    )
    extra = jnp.stack(
        [
            jnp.sum(grad_half.astype(jnp.float32), axis=(0, 1)),
            jnp.sum(upstream * normed, axis=(0, 1)),
            jnp.sum(upstream, axis=(0, 1)),
        ]
    )
    partial_value = jnp.concatenate([tap_grads, extra], axis=0)
    image_total = lax.psum(partial_value, "space")
    param_grads = lax.psum_scatter(image_total, "dp", scatter_dimension=1, tiled=True)
    return (input_grad[None], param_grads)


def solution(mesh):
    placed = (
        P("dp", "space", None, None),
        P("dp", "space", None, None),
        P("dp", "space", None),
        P("dp", "space", None),
        P("dp"),
        P(),
        P(),
        P(),
    )
    return jax.shard_map(
        body,
        mesh=mesh,
        in_specs=placed,
        out_specs=(P("dp", "space", None, None), P(None, "dp")),
        check_vma=False,
    )
```

profile of v0, /device:TPU:1, one launch (start us, length us, event | category | flops | bytes accessed | tf_op | source)
XLA Modules:
  0.0 1870.5 jit_solution(14623017093543364891)
XLA Ops:
  0.6 9.0 collective-permute-start.2
  9.6 8.6 collective-permute-start.3
  26.4 5.5 collective-permute-done.3
  38.1 4.3 reshape.126
  45.4 10.6 broadcast_add_fusion
  63.7 23.4 %fusion.57 = f32[7,7,3072]{2,1,0:T(8,128)S(1)} fusion(bf16[1,9,48,3072]{3,0,2,1:T(2,128)(2,1)} %copy-done.1, bf16[3,48,1,3072]{3,1,0,2:T(8,128)(2,1)S(1)} %fusion.43), kind=kOutput, calls=%fused_computation.69 | convolution fusion | flops 41803776 | bytes 4141056 | tf_op jit(solution)/shard_map/conv_general_dilated | solution.py:23
  96.3 681.4 %fusion = f32[52,16]{0,1:T(8,128)S(1)} fusion(f32[52,3072]{0,1:T(8,128)S(1)} %copy.47), kind=kCustom, calls=%all-reduce-scatter | all-reduce-scatter fusion | flops 212993 | bytes 646400
  779.0 126.9 %collective-permute-start.10 = (f32[52,16]{0,1:T(8,128)S(1)}, f32[52,16]{0,1:T(8,128)S(1)}, u32[]{:S(2)}, u32[]{:S(2)}) collective-permute-start(f32[52,16]{0,1:T(8,128)S(1)} %fusion), channel_id=1, source_target_pairs={{0,20},{4,24},{8,28},{12,32},{16,36},{20,40},{24,44},{28,48},{32,5... | collective-permute-start | bytes 9992
  906.0 23.7 %collective-permute-start.11 = (f32[52,16]{0,1:T(8,128)S(1)}, f32[52,16]{0,1:T(8,128)S(1)}, u32[]{:S(2)}, u32[]{:S(2)}) collective-permute-start(f32[52,16]{0,1:T(8,128)S(1)} %fusion), channel_id=1, source_target_pairs={{0,24},{4,28},{8,32},{12,36},{16,40},{20,44},{24,48},{28,52},{32,5... | collective-permute-start | bytes 9992
  929.7 23.7 %collective-permute-start.12 = (f32[52,16]{0,1:T(8,128)S(1)}, f32[52,16]{0,1:T(8,128)S(1)}, u32[]{:S(2)}, u32[]{:S(2)}) collective-permute-start(f32[52,16]{0,1:T(8,128)S(1)} %fusion), channel_id=1, source_target_pairs={{0,28},{4,32},{8,36},{12,40},{16,44},{20,48},{24,52},{28,56},{32,6... | collective-permute-start | bytes 9992
  953.4 23.7 %collective-permute-start.13 = (f32[52,16]{0,1:T(8,128)S(1)}, f32[52,16]{0,1:T(8,128)S(1)}, u32[]{:S(2)}, u32[]{:S(2)}) collective-permute-start(f32[52,16]{0,1:T(8,128)S(1)} %fusion), channel_id=1, source_target_pairs={{0,32},{4,36},{8,40},{12,44},{16,48},{20,52},{24,56},{28,60},{32,6... | collective-permute-start | bytes 9992
  977.1 23.7 %collective-permute-start.14 = (f32[52,16]{0,1:T(8,128)S(1)}, f32[52,16]{0,1:T(8,128)S(1)}, u32[]{:S(2)}, u32[]{:S(2)}) collective-permute-start(f32[52,16]{0,1:T(8,128)S(1)} %fusion), channel_id=1, source_target_pairs={{0,36},{4,40},{8,44},{12,48},{16,52},{20,56},{24,60},{28,64},{32,6... | collective-permute-start | bytes 9992
  1000.8 23.7 %collective-permute-start.15 = (f32[52,16]{0,1:T(8,128)S(1)}, f32[52,16]{0,1:T(8,128)S(1)}, u32[]{:S(2)}, u32[]{:S(2)}) collective-permute-start(f32[52,16]{0,1:T(8,128)S(1)} %fusion), channel_id=1, source_target_pairs={{0,40},{4,44},{8,48},{12,52},{16,56},{20,60},{24,64},{28,68},{32,7... | collective-permute-start | bytes 9992
  1024.5 23.7 %collective-permute-start.16 = (f32[52,16]{0,1:T(8,128)S(1)}, f32[52,16]{0,1:T(8,128)S(1)}, u32[]{:S(2)}, u32[]{:S(2)}) collective-permute-start(f32[52,16]{0,1:T(8,128)S(1)} %fusion), channel_id=1, source_target_pairs={{0,44},{4,48},{8,52},{12,56},{16,60},{20,64},{24,68},{28,72},{32,7... | collective-permute-start | bytes 9992
  1048.3 23.7 %collective-permute-start.17 = (f32[52,16]{0,1:T(8,128)S(1)}, f32[52,16]{0,1:T(8,128)S(1)}, u32[]{:S(2)}, u32[]{:S(2)}) collective-permute-start(f32[52,16]{0,1:T(8,128)S(1)} %fusion), channel_id=1, source_target_pairs={{0,48},{4,52},{8,56},{12,60},{16,64},{20,68},{24,72},{28,76},{32,8... | collective-permute-start | bytes 9992
  1072.0 23.7 %collective-permute-start.18 = (f32[52,16]{0,1:T(8,128)S(1)}, f32[52,16]{0,1:T(8,128)S(1)}, u32[]{:S(2)}, u32[]{:S(2)}) collective-permute-start(f32[52,16]{0,1:T(8,128)S(1)} %fusion), channel_id=1, source_target_pairs={{0,52},{4,56},{8,60},{12,64},{16,68},{20,72},{24,76},{28,80},{32,8... | collective-permute-start | bytes 9992
  1095.7 23.7 %collective-permute-start.19 = (f32[52,16]{0,1:T(8,128)S(1)}, f32[52,16]{0,1:T(8,128)S(1)}, u32[]{:S(2)}, u32[]{:S(2)}) collective-permute-start(f32[52,16]{0,1:T(8,128)S(1)} %fusion), channel_id=1, source_target_pairs={{0,56},{4,60},{8,64},{12,68},{16,72},{20,76},{24,80},{28,84},{32,8... | collective-permute-start | bytes 9992
  1119.4 23.7 %collective-permute-start.20 = (f32[52,16]{0,1:T(8,128)S(1)}, f32[52,16]{0,1:T(8,128)S(1)}, u32[]{:S(2)}, u32[]{:S(2)}) collective-permute-start(f32[52,16]{0,1:T(8,128)S(1)} %fusion), channel_id=1, source_target_pairs={{0,60},{4,64},{8,68},{12,72},{16,76},{20,80},{24,84},{28,88},{32,9... | collective-permute-start | bytes 9992
  1143.1 23.7 %collective-permute-start.21 = (f32[52,16]{0,1:T(8,128)S(1)}, f32[52,16]{0,1:T(8,128)S(1)}, u32[]{:S(2)}, u32[]{:S(2)}) collective-permute-start(f32[52,16]{0,1:T(8,128)S(1)} %fusion), channel_id=1, source_target_pairs={{0,64},{4,68},{8,72},{12,76},{16,80},{20,84},{24,88},{28,92},{32,9... | collective-permute-start | bytes 9992
  1166.9 23.7 %collective-permute-start.22 = (f32[52,16]{0,1:T(8,128)S(1)}, f32[52,16]{0,1:T(8,128)S(1)}, u32[]{:S(2)}, u32[]{:S(2)}) collective-permute-start(f32[52,16]{0,1:T(8,128)S(1)} %fusion), channel_id=1, source_target_pairs={{0,68},{4,72},{8,76},{12,80},{16,84},{20,88},{24,92},{28,96},{32,1... | collective-permute-start | bytes 9992
  1190.6 23.7 %collective-permute-start.23 = (f32[52,16]{0,1:T(8,128)S(1)}, f32[52,16]{0,1:T(8,128)S(1)}, u32[]{:S(2)}, u32[]{:S(2)}) collective-permute-start(f32[52,16]{0,1:T(8,128)S(1)} %fusion), channel_id=1, source_target_pairs={{0,72},{4,76},{8,80},{12,84},{16,88},{20,92},{24,96},{28,100},{32,... | collective-permute-start | bytes 9992
  1214.3 23.7 %collective-permute-start.24 = (f32[52,16]{0,1:T(8,128)S(1)}, f32[52,16]{0,1:T(8,128)S(1)}, u32[]{:S(2)}, u32[]{:S(2)}) collective-permute-start(f32[52,16]{0,1:T(8,128)S(1)} %fusion), channel_id=1, source_target_pairs={{0,76},{4,80},{8,84},{12,88},{16,92},{20,96},{24,100},{28,104},{32... | collective-permute-start | bytes 9992
  1238.0 23.7 %collective-permute-start.25 = (f32[52,16]{0,1:T(8,128)S(1)}, f32[52,16]{0,1:T(8,128)S(1)}, u32[]{:S(2)}, u32[]{:S(2)}) collective-permute-start(f32[52,16]{0,1:T(8,128)S(1)} %fusion), channel_id=1, source_target_pairs={{0,80},{4,84},{8,88},{12,92},{16,96},{20,100},{24,104},{28,108},{3... | collective-permute-start | bytes 9992
  1261.7 23.7 %collective-permute-start.26 = (f32[52,16]{0,1:T(8,128)S(1)}, f32[52,16]{0,1:T(8,128)S(1)}, u32[]{:S(2)}, u32[]{:S(2)}) collective-permute-start(f32[52,16]{0,1:T(8,128)S(1)} %fusion), channel_id=1, source_target_pairs={{0,84},{4,88},{8,92},{12,96},{16,100},{20,104},{24,108},{28,112},{... | collective-permute-start | bytes 9992
  1285.4 23.7 %collective-permute-start.27 = (f32[52,16]{0,1:T(8,128)S(1)}, f32[52,16]{0,1:T(8,128)S(1)}, u32[]{:S(2)}, u32[]{:S(2)}) collective-permute-start(f32[52,16]{0,1:T(8,128)S(1)} %fusion), channel_id=1, source_target_pairs={{0,88},{4,92},{8,96},{12,100},{16,104},{20,108},{24,112},{28,116},... | collective-permute-start | bytes 9992
  1309.2 23.7 %collective-permute-start.28 = (f32[52,16]{0,1:T(8,128)S(1)}, f32[52,16]{0,1:T(8,128)S(1)}, u32[]{:S(2)}, u32[]{:S(2)}) collective-permute-start(f32[52,16]{0,1:T(8,128)S(1)} %fusion), channel_id=1, source_target_pairs={{0,92},{4,96},{8,100},{12,104},{16,108},{20,112},{24,116},{28,120}... | collective-permute-start | bytes 9992
  1332.9 23.7 %collective-permute-start.29 = (f32[52,16]{0,1:T(8,128)S(1)}, f32[52,16]{0,1:T(8,128)S(1)}, u32[]{:S(2)}, u32[]{:S(2)}) collective-permute-start(f32[52,16]{0,1:T(8,128)S(1)} %fusion), channel_id=1, source_target_pairs={{0,96},{4,100},{8,104},{12,108},{16,112},{20,116},{24,120},{28,124... | collective-permute-start | bytes 9992
  1356.6 23.7 %collective-permute-start.30 = (f32[52,16]{0,1:T(8,128)S(1)}, f32[52,16]{0,1:T(8,128)S(1)}, u32[]{:S(2)}, u32[]{:S(2)}) collective-permute-start(f32[52,16]{0,1:T(8,128)S(1)} %fusion), channel_id=1, source_target_pairs={{0,100},{4,104},{8,108},{12,112},{16,116},{20,120},{24,124},{28,12... | collective-permute-start | bytes 9992
  1380.3 23.7 %collective-permute-start.31 = (f32[52,16]{0,1:T(8,128)S(1)}, f32[52,16]{0,1:T(8,128)S(1)}, u32[]{:S(2)}, u32[]{:S(2)}) collective-permute-start(f32[52,16]{0,1:T(8,128)S(1)} %fusion), channel_id=1, source_target_pairs={{0,104},{4,108},{8,112},{12,116},{16,120},{20,124},{24,128},{28,13... | collective-permute-start | bytes 9992
  1404.0 23.7 %collective-permute-start.32 = (f32[52,16]{0,1:T(8,128)S(1)}, f32[52,16]{0,1:T(8,128)S(1)}, u32[]{:S(2)}, u32[]{:S(2)}) collective-permute-start(f32[52,16]{0,1:T(8,128)S(1)} %fusion), channel_id=1, source_target_pairs={{0,108},{4,112},{8,116},{12,120},{16,124},{20,128},{24,132},{28,13... | collective-permute-start | bytes 9992
  1427.7 23.7 %collective-permute-start.33 = (f32[52,16]{0,1:T(8,128)S(1)}, f32[52,16]{0,1:T(8,128)S(1)}, u32[]{:S(2)}, u32[]{:S(2)}) collective-permute-start(f32[52,16]{0,1:T(8,128)S(1)} %fusion), channel_id=1, source_target_pairs={{0,112},{4,116},{8,120},{12,124},{16,128},{20,132},{24,136},{28,14... | collective-permute-start | bytes 9992
  1451.5 23.7 %collective-permute-start.34 = (f32[52,16]{0,1:T(8,128)S(1)}, f32[52,16]{0,1:T(8,128)S(1)}, u32[]{:S(2)}, u32[]{:S(2)}) collective-permute-start(f32[52,16]{0,1:T(8,128)S(1)} %fusion), channel_id=1, source_target_pairs={{0,116},{4,120},{8,124},{12,128},{16,132},{20,136},{24,140},{28,14... | collective-permute-start | bytes 9992
  1475.2 23.7 %collective-permute-start.35 = (f32[52,16]{0,1:T(8,128)S(1)}, f32[52,16]{0,1:T(8,128)S(1)}, u32[]{:S(2)}, u32[]{:S(2)}) collective-permute-start(f32[52,16]{0,1:T(8,128)S(1)} %fusion), channel_id=1, source_target_pairs={{0,120},{4,124},{8,128},{12,132},{16,136},{20,140},{24,144},{28,14... | collective-permute-start | bytes 9992
  1498.9 23.7 %collective-permute-start.36 = (f32[52,16]{0,1:T(8,128)S(1)}, f32[52,16]{0,1:T(8,128)S(1)}, u32[]{:S(2)}, u32[]{:S(2)}) collective-permute-start(f32[52,16]{0,1:T(8,128)S(1)} %fusion), channel_id=1, source_target_pairs={{0,124},{4,128},{8,132},{12,136},{16,140},{20,144},{24,148},{28,15... | collective-permute-start | bytes 9992
  1522.6 23.7 %collective-permute-start.37 = (f32[52,16]{0,1:T(8,128)S(1)}, f32[52,16]{0,1:T(8,128)S(1)}, u32[]{:S(2)}, u32[]{:S(2)}) collective-permute-start(f32[52,16]{0,1:T(8,128)S(1)} %fusion), channel_id=1, source_target_pairs={{0,128},{4,132},{8,136},{12,140},{16,144},{20,148},{24,152},{28,15... | collective-permute-start | bytes 9992
  1546.3 23.7 %collective-permute-start.38 = (f32[52,16]{0,1:T(8,128)S(1)}, f32[52,16]{0,1:T(8,128)S(1)}, u32[]{:S(2)}, u32[]{:S(2)}) collective-permute-start(f32[52,16]{0,1:T(8,128)S(1)} %fusion), channel_id=1, source_target_pairs={{0,132},{4,136},{8,140},{12,144},{16,148},{20,152},{24,156},{28,16... | collective-permute-start | bytes 9992
  1570.1 7.6 collective-permute-start.39
  1577.6 7.8 collective-permute-start.40
  1585.5 6.0 collective-permute-start.41
  1591.5 7.6 collective-permute-start.42
  1599.1 4.5 collective-permute-start.43
  1603.7 6.4 collective-permute-start.44
  1614.8 8.1 collective-permute-start.47
  1624.2 4.3 collective-permute-start.49
  1630.8 4.4 collective-permute-start.51
  1643.2 5.9 collective-permute-start.55
  1653.8 5.0 collective-permute-start.58
  1658.8 3.6 collective-permute-start.59
  1662.4 17.5 collective-permute-start.6
  1679.9 9.7 collective-permute-start.60
  1689.6 9.6 collective-permute-start.61
  1699.2 6.9 collective-permute-start.62
  1706.2 6.7 collective-permute-start.63
  1718.8 5.2 collective-permute-start.66
  1730.9 13.7 collective-permute-start.7
  1744.6 7.6 collective-permute-start.4
  1752.2 5.0 collective-permute-start.5
  1757.2 20.6 %collective-permute-start.8 = (f32[52,16]{0,1:T(8,128)S(1)}, f32[52,16]{0,1:T(8,128)S(1)}, u32[]{:S(2)}, u32[]{:S(2)}) collective-permute-start(f32[52,16]{0,1:T(8,128)S(1)} %fusion), channel_id=1, source_target_pairs={{0,12},{4,16},{8,20},{12,24},{16,28},{20,32},{24,36},{28,40},{32,4... | collective-permute-start | bytes 9992
  1778.6 25.9 %collective-permute-start.9 = (f32[52,16]{0,1:T(8,128)S(1)}, f32[52,16]{0,1:T(8,128)S(1)}, u32[]{:S(2)}, u32[]{:S(2)}) collective-permute-start(f32[52,16]{0,1:T(8,128)S(1)} %fusion), channel_id=1, source_target_pairs={{0,16},{4,20},{8,24},{12,28},{16,32},{20,36},{24,40},{28,44},{32,4... | collective-permute-start | bytes 9992
  1804.5 7.6 rev.3
  1814.1 7.1 concatenate.18
  1821.2 18.2 psum.8
  1848.2 3.8 reshape.135
  1855.0 9.7 fusion.17
  (150 shorter events, 87.8 us)
Async XLA Ops:
  0.6 22.8 %collective-permute-start.2 = (bf16[1,3,48,3072]{3,2,1,0:T(8,128)(2,1)}, bf16[1,3,48,3072]{3,2,1,0:T(8,128)(2,1)S(1)}, u32[]{:S(2)}, u32[]{:S(2)}) collective-permute-start(bf16[1,3,48,3072]{3,2,1,0:T(8,128)(2,1)} %param.8), channel_id=1, source_target_pairs={{0,1},{1,2},{2,3},{4,5},{5,6},{6,7},{8,9},{9,10},{10,11},{12,13},{... | collective-permute-start | bytes 2654216 | tf_op jit(solution)/shard_map/ppermute | solution.py:14
  9.6 22.2 %collective-permute-start.3 = (bf16[1,3,48,3072]{3,2,1,0:T(8,128)(2,1)}, bf16[1,3,48,3072]{3,2,1,0:T(8,128)(2,1)S(1)}, u32[]{:S(2)}, u32[]{:S(2)}) collective-permute-start(bf16[1,3,48,3072]{3,2,1,0:T(8,128)(2,1)} %param.8), channel_id=1, source_target_pairs={{1,0},{2,1},{3,2},{5,4},{6,5},{7,6},{9,8},{10,9},{11,10},{13,12},{... | collective-permute-start | bytes 2654216 | tf_op jit(solution)/shard_map/ppermute | solution.py:17
  18.2 1821.3 %collective-permute-start = (bf16[1,155,3072]{2,1,0:T(8,128)(2,1)}, bf16[1,155,3072]{2,1,0:T(8,128)(2,1)}, u32[]{:S(2)}, u32[]{:S(2)}) collective-permute-start(bf16[1,155,3072]{2,1,0:T(8,128)(2,1)} %param.10), channel_id=1, source_target_pairs={{0,1},{1,2},{2,3},{4,5},{5,6},{6,7},{8,9},{9,10},{10,11},{12,13},{... | collective-permute-start | bytes 2856968 | tf_op jit(solution)/shard_map/ppermute | solution.py:14
  20.1 1819.3 %collective-permute-start.1 = (bf16[1,155,3072]{2,1,0:T(8,128)(2,1)}, bf16[1,155,3072]{2,1,0:T(8,128)(2,1)}, u32[]{:S(2)}, u32[]{:S(2)}) collective-permute-start(bf16[1,155,3072]{2,1,0:T(8,128)(2,1)} %param.10), channel_id=1, source_target_pairs={{1,0},{2,1},{3,2},{5,4},{6,5},{7,6},{9,8},{10,9},{11,10},{13,12},{... | collective-permute-start | bytes 2856968 | tf_op jit(solution)/shard_map/ppermute | solution.py:17
  777.7 151.9 %collective-permute-start.69 = (f32[52,12]{0,1:T(8,128)S(1)}, f32[52,12]{0,1:T(8,128)S(1)}, u32[]{:S(2)}, u32[]{:S(2)}) collective-permute-start(f32[52,12]{0,1:T(8,128)S(1)} %slice.12), channel_id=1, source_target_pairs={{0,256},{4,260},{8,264},{12,268},{16,272},{20,276},{24,280},{28,28... | collective-permute-start | bytes 7496
  779.0 174.4 %collective-permute-start.10 = (f32[52,16]{0,1:T(8,128)S(1)}, f32[52,16]{0,1:T(8,128)S(1)}, u32[]{:S(2)}, u32[]{:S(2)}) collective-permute-start(f32[52,16]{0,1:T(8,128)S(1)} %fusion), channel_id=1, source_target_pairs={{0,20},{4,24},{8,28},{12,32},{16,36},{20,40},{24,44},{28,48},{32,5... | collective-permute-start | bytes 9992
  906.0 71.1 %collective-permute-start.11 = (f32[52,16]{0,1:T(8,128)S(1)}, f32[52,16]{0,1:T(8,128)S(1)}, u32[]{:S(2)}, u32[]{:S(2)}) collective-permute-start(f32[52,16]{0,1:T(8,128)S(1)} %fusion), channel_id=1, source_target_pairs={{0,24},{4,28},{8,32},{12,36},{16,40},{20,44},{24,48},{28,52},{32,5... | collective-permute-start | bytes 9992
  929.7 71.1 %collective-permute-start.12 = (f32[52,16]{0,1:T(8,128)S(1)}, f32[52,16]{0,1:T(8,128)S(1)}, u32[]{:S(2)}, u32[]{:S(2)}) collective-permute-start(f32[52,16]{0,1:T(8,128)S(1)} %fusion), channel_id=1, source_target_pairs={{0,28},{4,32},{8,36},{12,40},{16,44},{20,48},{24,52},{28,56},{32,6... | collective-permute-start | bytes 9992
  953.4 71.1 %collective-permute-start.13 = (f32[52,16]{0,1:T(8,128)S(1)}, f32[52,16]{0,1:T(8,128)S(1)}, u32[]{:S(2)}, u32[]{:S(2)}) collective-permute-start(f32[52,16]{0,1:T(8,128)S(1)} %fusion), channel_id=1, source_target_pairs={{0,32},{4,36},{8,40},{12,44},{16,48},{20,52},{24,56},{28,60},{32,6... | collective-permute-start | bytes 9992
  977.1 71.1 %collective-permute-start.14 = (f32[52,16]{0,1:T(8,128)S(1)}, f32[52,16]{0,1:T(8,128)S(1)}, u32[]{:S(2)}, u32[]{:S(2)}) collective-permute-start(f32[52,16]{0,1:T(8,128)S(1)} %fusion), channel_id=1, source_target_pairs={{0,36},{4,40},{8,44},{12,48},{16,52},{20,56},{24,60},{28,64},{32,6... | collective-permute-start | bytes 9992
  1000.8 71.1 %collective-permute-start.15 = (f32[52,16]{0,1:T(8,128)S(1)}, f32[52,16]{0,1:T(8,128)S(1)}, u32[]{:S(2)}, u32[]{:S(2)}) collective-permute-start(f32[52,16]{0,1:T(8,128)S(1)} %fusion), channel_id=1, source_target_pairs={{0,40},{4,44},{8,48},{12,52},{16,56},{20,60},{24,64},{28,68},{32,7... | collective-permute-start | bytes 9992
  1024.5 71.1 %collective-permute-start.16 = (f32[52,16]{0,1:T(8,128)S(1)}, f32[52,16]{0,1:T(8,128)S(1)}, u32[]{:S(2)}, u32[]{:S(2)}) collective-permute-start(f32[52,16]{0,1:T(8,128)S(1)} %fusion), channel_id=1, source_target_pairs={{0,44},{4,48},{8,52},{12,56},{16,60},{20,64},{24,68},{28,72},{32,7... | collective-permute-start | bytes 9992
  1048.3 71.1 %collective-permute-start.17 = (f32[52,16]{0,1:T(8,128)S(1)}, f32[52,16]{0,1:T(8,128)S(1)}, u32[]{:S(2)}, u32[]{:S(2)}) collective-permute-start(f32[52,16]{0,1:T(8,128)S(1)} %fusion), channel_id=1, source_target_pairs={{0,48},{4,52},{8,56},{12,60},{16,64},{20,68},{24,72},{28,76},{32,8... | collective-permute-start | bytes 9992
  1072.0 71.1 %collective-permute-start.18 = (f32[52,16]{0,1:T(8,128)S(1)}, f32[52,16]{0,1:T(8,128)S(1)}, u32[]{:S(2)}, u32[]{:S(2)}) collective-permute-start(f32[52,16]{0,1:T(8,128)S(1)} %fusion), channel_id=1, source_target_pairs={{0,52},{4,56},{8,60},{12,64},{16,68},{20,72},{24,76},{28,80},{32,8... | collective-permute-start | bytes 9992
  1095.7 71.1 %collective-permute-start.19 = (f32[52,16]{0,1:T(8,128)S(1)}, f32[52,16]{0,1:T(8,128)S(1)}, u32[]{:S(2)}, u32[]{:S(2)}) collective-permute-start(f32[52,16]{0,1:T(8,128)S(1)} %fusion), channel_id=1, source_target_pairs={{0,56},{4,60},{8,64},{12,68},{16,72},{20,76},{24,80},{28,84},{32,8... | collective-permute-start | bytes 9992
  1119.4 71.1 %collective-permute-start.20 = (f32[52,16]{0,1:T(8,128)S(1)}, f32[52,16]{0,1:T(8,128)S(1)}, u32[]{:S(2)}, u32[]{:S(2)}) collective-permute-start(f32[52,16]{0,1:T(8,128)S(1)} %fusion), channel_id=1, source_target_pairs={{0,60},{4,64},{8,68},{12,72},{16,76},{20,80},{24,84},{28,88},{32,9... | collective-permute-start | bytes 9992
  1143.1 71.1 %collective-permute-start.21 = (f32[52,16]{0,1:T(8,128)S(1)}, f32[52,16]{0,1:T(8,128)S(1)}, u32[]{:S(2)}, u32[]{:S(2)}) collective-permute-start(f32[52,16]{0,1:T(8,128)S(1)} %fusion), channel_id=1, source_target_pairs={{0,64},{4,68},{8,72},{12,76},{16,80},{20,84},{24,88},{28,92},{32,9... | collective-permute-start | bytes 9992
  1166.9 71.1 %collective-permute-start.22 = (f32[52,16]{0,1:T(8,128)S(1)}, f32[52,16]{0,1:T(8,128)S(1)}, u32[]{:S(2)}, u32[]{:S(2)}) collective-permute-start(f32[52,16]{0,1:T(8,128)S(1)} %fusion), channel_id=1, source_target_pairs={{0,68},{4,72},{8,76},{12,80},{16,84},{20,88},{24,92},{28,96},{32,1... | collective-permute-start | bytes 9992
  1190.6 71.1 %collective-permute-start.23 = (f32[52,16]{0,1:T(8,128)S(1)}, f32[52,16]{0,1:T(8,128)S(1)}, u32[]{:S(2)}, u32[]{:S(2)}) collective-permute-start(f32[52,16]{0,1:T(8,128)S(1)} %fusion), channel_id=1, source_target_pairs={{0,72},{4,76},{8,80},{12,84},{16,88},{20,92},{24,96},{28,100},{32,... | collective-permute-start | bytes 9992
  1214.3 71.1 %collective-permute-start.24 = (f32[52,16]{0,1:T(8,128)S(1)}, f32[52,16]{0,1:T(8,128)S(1)}, u32[]{:S(2)}, u32[]{:S(2)}) collective-permute-start(f32[52,16]{0,1:T(8,128)S(1)} %fusion), channel_id=1, source_target_pairs={{0,76},{4,80},{8,84},{12,88},{16,92},{20,96},{24,100},{28,104},{32... | collective-permute-start | bytes 9992
  1238.0 71.1 %collective-permute-start.25 = (f32[52,16]{0,1:T(8,128)S(1)}, f32[52,16]{0,1:T(8,128)S(1)}, u32[]{:S(2)}, u32[]{:S(2)}) collective-permute-start(f32[52,16]{0,1:T(8,128)S(1)} %fusion), channel_id=1, source_target_pairs={{0,80},{4,84},{8,88},{12,92},{16,96},{20,100},{24,104},{28,108},{3... | collective-permute-start | bytes 9992
  1261.7 71.1 %collective-permute-start.26 = (f32[52,16]{0,1:T(8,128)S(1)}, f32[52,16]{0,1:T(8,128)S(1)}, u32[]{:S(2)}, u32[]{:S(2)}) collective-permute-start(f32[52,16]{0,1:T(8,128)S(1)} %fusion), channel_id=1, source_target_pairs={{0,84},{4,88},{8,92},{12,96},{16,100},{20,104},{24,108},{28,112},{... | collective-permute-start | bytes 9992
  1285.4 71.1 %collective-permute-start.27 = (f32[52,16]{0,1:T(8,128)S(1)}, f32[52,16]{0,1:T(8,128)S(1)}, u32[]{:S(2)}, u32[]{:S(2)}) collective-permute-start(f32[52,16]{0,1:T(8,128)S(1)} %fusion), channel_id=1, source_target_pairs={{0,88},{4,92},{8,96},{12,100},{16,104},{20,108},{24,112},{28,116},... | collective-permute-start | bytes 9992
  1309.2 71.1 %collective-permute-start.28 = (f32[52,16]{0,1:T(8,128)S(1)}, f32[52,16]{0,1:T(8,128)S(1)}, u32[]{:S(2)}, u32[]{:S(2)}) collective-permute-start(f32[52,16]{0,1:T(8,128)S(1)} %fusion), channel_id=1, source_target_pairs={{0,92},{4,96},{8,100},{12,104},{16,108},{20,112},{24,116},{28,120}... | collective-permute-start | bytes 9992
  1332.9 71.1 %collective-permute-start.29 = (f32[52,16]{0,1:T(8,128)S(1)}, f32[52,16]{0,1:T(8,128)S(1)}, u32[]{:S(2)}, u32[]{:S(2)}) collective-permute-start(f32[52,16]{0,1:T(8,128)S(1)} %fusion), channel_id=1, source_target_pairs={{0,96},{4,100},{8,104},{12,108},{16,112},{20,116},{24,120},{28,124... | collective-permute-start | bytes 9992
  1356.6 71.1 %collective-permute-start.30 = (f32[52,16]{0,1:T(8,128)S(1)}, f32[52,16]{0,1:T(8,128)S(1)}, u32[]{:S(2)}, u32[]{:S(2)}) collective-permute-start(f32[52,16]{0,1:T(8,128)S(1)} %fusion), channel_id=1, source_target_pairs={{0,100},{4,104},{8,108},{12,112},{16,116},{20,120},{24,124},{28,12... | collective-permute-start | bytes 9992
  1380.3 71.1 %collective-permute-start.31 = (f32[52,16]{0,1:T(8,128)S(1)}, f32[52,16]{0,1:T(8,128)S(1)}, u32[]{:S(2)}, u32[]{:S(2)}) collective-permute-start(f32[52,16]{0,1:T(8,128)S(1)} %fusion), channel_id=1, source_target_pairs={{0,104},{4,108},{8,112},{12,116},{16,120},{20,124},{24,128},{28,13... | collective-permute-start | bytes 9992
  1404.0 71.1 %collective-permute-start.32 = (f32[52,16]{0,1:T(8,128)S(1)}, f32[52,16]{0,1:T(8,128)S(1)}, u32[]{:S(2)}, u32[]{:S(2)}) collective-permute-start(f32[52,16]{0,1:T(8,128)S(1)} %fusion), channel_id=1, source_target_pairs={{0,108},{4,112},{8,116},{12,120},{16,124},{20,128},{24,132},{28,13... | collective-permute-start | bytes 9992
  1427.7 71.1 %collective-permute-start.33 = (f32[52,16]{0,1:T(8,128)S(1)}, f32[52,16]{0,1:T(8,128)S(1)}, u32[]{:S(2)}, u32[]{:S(2)}) collective-permute-start(f32[52,16]{0,1:T(8,128)S(1)} %fusion), channel_id=1, source_target_pairs={{0,112},{4,116},{8,120},{12,124},{16,128},{20,132},{24,136},{28,14... | collective-permute-start | bytes 9992
  1451.5 71.1 %collective-permute-start.34 = (f32[52,16]{0,1:T(8,128)S(1)}, f32[52,16]{0,1:T(8,128)S(1)}, u32[]{:S(2)}, u32[]{:S(2)}) collective-permute-start(f32[52,16]{0,1:T(8,128)S(1)} %fusion), channel_id=1, source_target_pairs={{0,116},{4,120},{8,124},{12,128},{16,132},{20,136},{24,140},{28,14... | collective-permute-start | bytes 9992
  1475.2 71.1 %collective-permute-start.35 = (f32[52,16]{0,1:T(8,128)S(1)}, f32[52,16]{0,1:T(8,128)S(1)}, u32[]{:S(2)}, u32[]{:S(2)}) collective-permute-start(f32[52,16]{0,1:T(8,128)S(1)} %fusion), channel_id=1, source_target_pairs={{0,120},{4,124},{8,128},{12,132},{16,136},{20,140},{24,144},{28,14... | collective-permute-start | bytes 9992
  1498.9 71.1 %collective-permute-start.36 = (f32[52,16]{0,1:T(8,128)S(1)}, f32[52,16]{0,1:T(8,128)S(1)}, u32[]{:S(2)}, u32[]{:S(2)}) collective-permute-start(f32[52,16]{0,1:T(8,128)S(1)} %fusion), channel_id=1, source_target_pairs={{0,124},{4,128},{8,132},{12,136},{16,140},{20,144},{24,148},{28,15... | collective-permute-start | bytes 9992
  1522.6 55.0 %collective-permute-start.37 = (f32[52,16]{0,1:T(8,128)S(1)}, f32[52,16]{0,1:T(8,128)S(1)}, u32[]{:S(2)}, u32[]{:S(2)}) collective-permute-start(f32[52,16]{0,1:T(8,128)S(1)} %fusion), channel_id=1, source_target_pairs={{0,128},{4,132},{8,136},{12,140},{16,144},{20,148},{24,152},{28,15... | collective-permute-start | bytes 9992
  1546.3 39.1 %collective-permute-start.38 = (f32[52,16]{0,1:T(8,128)S(1)}, f32[52,16]{0,1:T(8,128)S(1)}, u32[]{:S(2)}, u32[]{:S(2)}) collective-permute-start(f32[52,16]{0,1:T(8,128)S(1)} %fusion), channel_id=1, source_target_pairs={{0,132},{4,136},{8,140},{12,144},{16,148},{20,152},{24,156},{28,16... | collective-permute-start | bytes 9992
  1570.1 21.5 %collective-permute-start.39 = (f32[52,16]{0,1:T(8,128)S(1)}, f32[52,16]{0,1:T(8,128)S(1)}, u32[]{:S(2)}, u32[]{:S(2)}) collective-permute-start(f32[52,16]{0,1:T(8,128)S(1)} %fusion), channel_id=1, source_target_pairs={{0,136},{4,140},{8,144},{12,148},{16,152},{20,156},{24,160},{28,16... | collective-permute-start | bytes 9992
  1577.6 21.5 %collective-permute-start.40 = (f32[52,16]{0,1:T(8,128)S(1)}, f32[52,16]{0,1:T(8,128)S(1)}, u32[]{:S(2)}, u32[]{:S(2)}) collective-permute-start(f32[52,16]{0,1:T(8,128)S(1)} %fusion), channel_id=1, source_target_pairs={{0,140},{4,144},{8,148},{12,152},{16,156},{20,160},{24,164},{28,16... | collective-permute-start | bytes 9992
  1585.5 18.2 collective-permute-start.41
  1591.5 18.5 collective-permute-start.42
  1599.1 13.0 collective-permute-start.43
  1603.7 11.1 collective-permute-start.44
  1610.1 12.8 collective-permute-start.45
  1612.1 12.1 collective-permute-start.46
  1614.8 13.7 collective-permute-start.47
  1624.2 11.0 collective-permute-start.49
  1638.7 10.4 collective-permute-start.53
  1640.8 11.2 collective-permute-start.54
  1643.2 10.6 collective-permute-start.55
  1653.8 26.1 %collective-permute-start.58 = (f32[52,16]{0,1:T(8,128)S(1)}, f32[52,16]{0,1:T(8,128)S(1)}, u32[]{:S(2)}, u32[]{:S(2)}) collective-permute-start(f32[52,16]{0,1:T(8,128)S(1)} %fusion), channel_id=1, source_target_pairs={{0,212},{4,216},{8,220},{12,224},{16,228},{20,232},{24,236},{28,24... | collective-permute-start | bytes 9992
  1658.8 30.8 %collective-permute-start.59 = (f32[52,16]{0,1:T(8,128)S(1)}, f32[52,16]{0,1:T(8,128)S(1)}, u32[]{:S(2)}, u32[]{:S(2)}) collective-permute-start(f32[52,16]{0,1:T(8,128)S(1)} %fusion), channel_id=1, source_target_pairs={{0,216},{4,220},{8,224},{12,228},{16,232},{20,236},{24,240},{28,24... | collective-permute-start | bytes 9992
  1662.4 36.9 %collective-permute-start.6 = (f32[52,16]{0,1:T(8,128)S(1)}, f32[52,16]{0,1:T(8,128)S(1)}, u32[]{:S(2)}, u32[]{:S(2)}) collective-permute-start(f32[52,16]{0,1:T(8,128)S(1)} %fusion), channel_id=1, source_target_pairs={{0,4},{4,8},{8,12},{12,16},{16,20},{20,24},{24,28},{28,32},{32,36}... | collective-permute-start | bytes 9992
  1679.9 26.3 %collective-permute-start.60 = (f32[52,16]{0,1:T(8,128)S(1)}, f32[52,16]{0,1:T(8,128)S(1)}, u32[]{:S(2)}, u32[]{:S(2)}) collective-permute-start(f32[52,16]{0,1:T(8,128)S(1)} %fusion), channel_id=1, source_target_pairs={{0,220},{4,224},{8,228},{12,232},{16,236},{20,240},{24,244},{28,24... | collective-permute-start | bytes 9992
  1689.6 23.3 %collective-permute-start.61 = (f32[52,16]{0,1:T(8,128)S(1)}, f32[52,16]{0,1:T(8,128)S(1)}, u32[]{:S(2)}, u32[]{:S(2)}) collective-permute-start(f32[52,16]{0,1:T(8,128)S(1)} %fusion), channel_id=1, source_target_pairs={{0,224},{4,228},{8,232},{12,236},{16,240},{20,244},{24,248},{28,25... | collective-permute-start | bytes 9992
  1699.2 16.5 collective-permute-start.62
  1706.2 12.6 collective-permute-start.63
  1712.9 11.2 collective-permute-start.64
  1715.7 11.4 collective-permute-start.65
  1718.8 12.1 collective-permute-start.66
  1724.1 20.5 %collective-permute-start.67 = (f32[52,16]{0,1:T(8,128)S(1)}, f32[52,16]{0,1:T(8,128)S(1)}, u32[]{:S(2)}, u32[]{:S(2)}) collective-permute-start(f32[52,16]{0,1:T(8,128)S(1)} %fusion), channel_id=1, source_target_pairs={{0,248},{4,252},{8,256},{12,260},{16,264},{20,268},{24,272},{28,27... | collective-permute-start | bytes 9992
  1727.2 25.0 %collective-permute-start.68 = (f32[52,16]{0,1:T(8,128)S(1)}, f32[52,16]{0,1:T(8,128)S(1)}, u32[]{:S(2)}, u32[]{:S(2)}) collective-permute-start(f32[52,16]{0,1:T(8,128)S(1)} %fusion), channel_id=1, source_target_pairs={{0,252},{4,256},{8,260},{12,264},{16,268},{20,272},{24,276},{28,28... | collective-permute-start | bytes 9992
  1730.9 26.3 %collective-permute-start.7 = (f32[52,16]{0,1:T(8,128)S(1)}, f32[52,16]{0,1:T(8,128)S(1)}, u32[]{:S(2)}, u32[]{:S(2)}) collective-permute-start(f32[52,16]{0,1:T(8,128)S(1)} %fusion), channel_id=1, source_target_pairs={{0,8},{4,12},{8,16},{12,20},{16,24},{20,28},{24,32},{28,36},{32,40... | collective-permute-start | bytes 9992
  1744.6 99.2 %collective-permute-start.4 = (bf16[1,3,48,3072]{3,2,1,0:T(8,128)(2,1)}, bf16[1,3,48,3072]{3,2,1,0:T(8,128)(2,1)}, u32[]{:S(2)}, u32[]{:S(2)}) collective-permute-start(bf16[1,3,48,3072]{3,2,1,0:T(8,128)(2,1)} %get-tuple-element.9), channel_id=1, source_target_pairs={{0,1},{1,2},{2,3},{4,5},{5,6},{6,7},{8,9},{9,10},{10,11},{12,13},{... | collective-permute-start | bytes 2654216 | tf_op jit(solution)/shard_map/ppermute | solution.py:14
  1752.2 91.6 %collective-permute-start.5 = (bf16[1,3,48,3072]{3,2,1,0:T(8,128)(2,1)}, bf16[1,3,48,3072]{3,2,1,0:T(8,128)(2,1)}, u32[]{:S(2)}, u32[]{:S(2)}) collective-permute-start(bf16[1,3,48,3072]{3,2,1,0:T(8,128)(2,1)} %get-tuple-element.9), channel_id=1, source_target_pairs={{1,0},{2,1},{3,2},{5,4},{6,5},{7,6},{9,8},{10,9},{11,10},{13,12},{... | collective-permute-start | bytes 2654216 | tf_op jit(solution)/shard_map/ppermute | solution.py:17
  1757.2 21.4 %collective-permute-start.8 = (f32[52,16]{0,1:T(8,128)S(1)}, f32[52,16]{0,1:T(8,128)S(1)}, u32[]{:S(2)}, u32[]{:S(2)}) collective-permute-start(f32[52,16]{0,1:T(8,128)S(1)} %fusion), channel_id=1, source_target_pairs={{0,12},{4,16},{8,20},{12,24},{16,28},{20,32},{24,36},{28,40},{32,4... | collective-permute-start | bytes 9992
  1778.6 35.5 %collective-permute-start.9 = (f32[52,16]{0,1:T(8,128)S(1)}, f32[52,16]{0,1:T(8,128)S(1)}, u32[]{:S(2)}, u32[]{:S(2)}) collective-permute-start(f32[52,16]{0,1:T(8,128)S(1)} %fusion), channel_id=1, source_target_pairs={{0,16},{4,20},{8,24},{12,28},{16,32},{20,36},{24,40},{28,44},{32,4... | collective-permute-start | bytes 9992
  (18 other events, 3437.5 us)
where the time goes:
time: 1880 us; the launch traced here: 1870 us
  starting transfers between devices  1050 us (56%)
  blocking collectives  700 us (37%)
  local copies, waits for them, and re-layouts  57.4 us (3%)
  matrix products  43.7 us (2%)
    unnamed x64, starting transfers between devices  1010 us
    unnamed x1, blocking collectives  681 us
    conv_general_dilated x3, matrix products, grouped_conv(): lax.conv_general_dilated(lhs, rhs, (1, 1), ((0, 0), (col_pad, col_pad)),...  43.7 us
  transfers between devices with their start and end apart: 70, of which 2 were waited for; matrix products, arithmetic and copies ran while one was open for 41% of the time, Pallas kernels for 0%

commit v1 on v0

v1 whole, which is shorter than its diff:
```python
import functools

import jax
import jax.numpy as jnp
from jax import lax
from jax.experimental import pallas as pl
from jax.experimental.pallas import tpu as pltpu
from jax.sharding import PartitionSpec as P

KERNEL = 7
NX = 4
NY_LO = 4
LANES = 128
SEGS = 8
TAP_ROWS = 56
F32 = jnp.float32
BF16 = jnp.bfloat16


def fused(
    sizes, feat, ngrad, tok, tail, dk, place, valid, bias, gain, out_ig, out_pg,
    f_own, f_sib, f_cross, n_own, t_all, k_raw, g_own, g_sib, g_cross, o_own,
    f3, g3, n3, w8, mixed, resid, onehot, tmp, pacc, pg, ra, rb, sb, rc, sc, rd, sd, pf,
    local_sem, out_sem, fs_s, fs_r, fx_s, fx_r, gs_s, gs_r, gx_s, gx_r, t_s, t_r,
    a_s, a_r, b_s, b_r, c_s, c_r, d_s, d_r, e_s, e_r, h_s, h_r,
):
    nz, ny_lo, nx, nct, rows, cols, seq = sizes
    ny = 2 * ny_lo
    channels = nct * LANES
    segw = cols // SEGS
    wide = segw + KERNEL - 1
    per_y = 64 // ny
    halfct = nct // 2
    dp, s = lax.axis_index("dp"), lax.axis_index("space")
    x = lax.rem(dp, nx)
    y_lo = lax.rem(lax.div(dp, nx), ny_lo)
    z = lax.div(dp, nx * ny_lo)
    core = lax.rem(s, 2)
    y_hi = lax.div(s, 2)
    y = y_hi * ny_lo + y_lo
    m = core * nx + x
    has_cross = (s == 1) | (s == 2)
    no_cross = (s == 0) | (s == 3)

    def flip(i, n):
        return i + core * (n - 1 - 2 * i)

    def dev(z_, y_, x_, core_):
        hi = lax.div(y_, ny_lo)
        return ((z_ * ny_lo + lax.rem(y_, ny_lo)) * nx + x_, hi * 2 + core_)

    sib = (dp, s + 1 - 2 * core)
    cross = (dp, 3 - s)

    def remote(src, dst, ss, rs, device):
        return pltpu.make_async_remote_copy(
            src_ref=src, dst_ref=dst, send_sem=ss, recv_sem=rs,
            device_id=device, device_id_type=pl.DeviceIdType.MESH,
        )

    local = [pltpu.make_async_copy(dk, k_raw, local_sem.at[0])]
    for r in range(rows):
        local.append(pltpu.make_async_copy(feat.at[0, flip(r, rows)], f_own.at[r], local_sem.at[1 + r]))
        local.append(pltpu.make_async_copy(ngrad.at[0, flip(r, rows)], n_own.at[r], local_sem.at[4 + r]))
    local.append(pltpu.make_async_copy(tok.at[0, pl.ds(0, 144)], t_all.at[pl.ds(32, 144)], local_sem.at[7]))
    local.append(pltpu.make_async_copy(tail, t_all.at[pl.ds(176, 32)], local_sem.at[8]))
    for copy in local:
        copy.start()

    barrier = pltpu.get_barrier_semaphore()

    def greet(device):
        pl.semaphore_signal(barrier, inc=1, device_id=device, device_id_type=pl.DeviceIdType.MESH)

    @pl.when(has_cross)
    def _():
        greet(cross)

    for d in range(2 * nx - 1):
        dd = d + 1
        flat = lax.rem(core * nx + x + dd, 2 * nx)
        greet(dev(z, y, lax.rem(flat, nx), lax.div(flat, nx)))
    for d in range(1, ny):
        greet(dev(z, lax.rem(y + d, ny), x, core))
    for d in range(1, nz):
        greet(dev(lax.rem(z + d, nz), y, x, core))
    peers = 2 * nx - 1 + ny - 1 + nz - 1

    @pl.when(has_cross)
    def _():
        pl.semaphore_wait(barrier, peers + 1)

    @pl.when(no_cross)
    def _():
        pl.semaphore_wait(barrier, peers)

    fx = [remote(feat.at[0, flip(r, rows)], f_cross.at[r], fx_s.at[r], fx_r.at[r], cross) for r in range(rows)]
    fs = [remote(feat.at[0, flip(r, rows)], f_sib.at[r], fs_s.at[r], fs_r.at[r], sib) for r in range(rows)]
    t_next = remote(tail, t_all.at[pl.ds(0, 32)], t_s.at[0], t_r.at[0], (dp, s + 1))
    t_prev = remote(tok.at[0, pl.ds(0, 32)], t_all.at[pl.ds(208, 32)], t_s.at[1], t_r.at[1], (dp, s - 1))

    @pl.when(has_cross)
    def _():
        for r in range(rows):
            fx[r].start()

    for r in range(rows):
        fs[r].start()

    @pl.when(s < 3)
    def _():
        t_next.start()

    @pl.when(s > 0)
    def _():
        t_prev.start()

    @pl.when(no_cross)
    def _():
        f_cross[...] = jnp.zeros_like(f_cross)
        g_cross[...] = jnp.zeros_like(g_cross)

    @pl.when(s == 0)
    def _():
        t_all[pl.ds(0, 32), :] = jnp.zeros((32, channels), BF16)

    @pl.when(s == 3)
    def _():
        t_all[pl.ds(208, 32), :] = jnp.zeros((32, channels), BF16)

    tmp[...] = jnp.zeros_like(tmp)

    def lanes(ct):
        return pl.ds(pl.multiple_of(ct * LANES, LANES), LANES)

    def loop(body):
        lax.fori_loop(0, nct, lambda ct, c: (body(ct), c)[1], 0)

    local[0].wait()

    def spread(ct):
        taps = k_raw[:, :, lanes(ct)].astype(F32)
        for a in range(KERNEL):
            for b in range(KERNEL):
                row = pl.multiple_of((flip(a, KERNEL) * KERNEL + b) * 8, 8)
                w8[ct, pl.ds(row, 8), :] = jnp.broadcast_to(taps[a, b][None, :], (8, LANES))

    loop(spread)

    def weight(ct, a, b):
        return w8[ct, pl.ds((a * KERNEL + b) * 8, 8), :][None]

    def widen(src, row, dst, drow, slot):
        def body(ct):
            tmp[slot, pl.ds(8, cols), :] = src[row, :, lanes(ct)].astype(F32)
            for k in range(wide):
                dst[ct, drow, k] = tmp[slot, pl.ds(8 - KERNEL // 2 + k, SEGS, stride=segw), :]
        return body

    def both(*bodies):
        def body(ct):
            for one in bodies:
                one(ct)
        loop(body)

    for copy in local[1:7]:
        copy.wait()

    def stage_grad(ct):
        for r in range(rows):
            tmp[3 + r, pl.ds(8, cols), :] = n_own[r, :, lanes(ct)].astype(F32)
            for k in range(segw):
                n3[ct, r, k] = tmp[3 + r, pl.ds(8 + k, SEGS, stride=segw), :]

    both(*[widen(f_own, r, f3, 3 + r, r) for r in range(rows)], stage_grad)
    for r in range(rows):
        fs[r].wait_recv()
    both(*[widen(f_sib, r, f3, 8 - r, r) for r in range(rows)])

    def conv(ct, acc, source, combos, backward):
        for e in sorted({e for e, _ in combos}):
            line = source[ct, e]
            for r in range(rows):
                if (e, r) not in combos:
                    continue
                for b in range(KERNEL):
                    if backward:
                        acc[r] = acc[r] + weight(ct, KERNEL - 1 - (e - r), KERNEL - 1 - b) * line[b:b + segw]
                    else:
                        acc[r] = acc[r] + weight(ct, e - r, b) * line[b:b + segw]
        return acc

    all_combos = [(e, r) for e in range(rows + 6) for r in range(rows) if 0 <= e - r < KERNEL]
    near = [(e, r) for e, r in all_combos if e >= 3]

    def forward_near(ct):
        start = jnp.broadcast_to(bias[pl.ds(ct, 1), :][None], (segw, SEGS, LANES))
        acc = conv(ct, [start] * rows, f3, near, False)
        for r in range(rows):
            mixed[ct, r] = acc[r]

    loop(forward_near)

    local[7].wait()
    local[8].wait()

    @pl.when(s > 0)
    def _():
        t_next.wait_recv()

    @pl.when(s < 3)
    def _():
        t_prev.wait_recv()

    first = place[0, 0, 0] - s * seq
    held = valid[0] - s * rows
    width = t_all.shape[0]
    lane = lax.broadcasted_iota(jnp.int32, (SEGS, width), 1)
    seg = lax.broadcasted_iota(jnp.int32, (SEGS, width), 0)
    late = jnp.where(lane < 208, lane - 176 + (seq - 32), lane - 208 + seq)
    late = jnp.where(late < 144, -4096, late)
    position = jnp.where(lane < 176, lane - 32, late)
    for r in range(rows):
        row = flip(r, rows)
        base = jnp.where(row < held, first + row * (cols + 1), -8192)
        for k in range(segw):
            hit = position == base + segw * seg + k
            onehot[pl.ds((r * segw + k) * SEGS, SEGS), :] = jnp.where(hit, 1.0, 0.0).astype(F32)

    def pick(ct):
        found = jnp.dot(onehot[...].astype(BF16), t_all[:, lanes(ct)], preferred_element_type=F32)
        resid[ct] = found.reshape(rows, segw, SEGS, LANES)

    loop(pick)

    inv_c = 1.0 / channels
    gx = [remote(g_own.at[r], g_cross.at[r], gx_s.at[r], gx_r.at[r], cross) for r in range(rows)]
    gs = [remote(g_own.at[r], g_sib.at[r], gs_s.at[r], gs_r.at[r], sib) for r in range(rows)]

    def tap_rows(t):
        return pl.ds(t * 8, 8)

    for r in reversed(range(rows)):
        newest = r == rows - 1

        @pl.when(has_cross)
        def _(r=r):
            fx[2 - r].wait_recv()

        def forward_far(ct, r=r):
            widen(f_cross, 2 - r, f3, r, 0)(ct)
            acc = [mixed[ct, i] for i in range(rows)]
            acc = conv(ct, acc, f3, [(e, i) for e, i in all_combos if e == r], False)
            for i in range(r + 1):
                mixed[ct, i] = acc[i]

        loop(forward_far)
        zero = jnp.zeros((segw, SEGS, LANES), F32)

        def sums(ct, carry, r=r):
            total, scaled = carry
            return total + mixed[ct, r], scaled + n3[ct, r] * gain[pl.ds(ct, 1), :][None]

        total, scaled_sum = lax.fori_loop(0, nct, sums, (zero, zero))
        center = jnp.sum(total, axis=-1, keepdims=True) * inv_c
        scaled_mean = jnp.sum(scaled_sum, axis=-1, keepdims=True) * inv_c

        def moments(ct, carry, r=r, center=center):
            square, inner = carry
            offset = mixed[ct, r] - center
            return square + offset * offset, inner + offset * (n3[ct, r] * gain[pl.ds(ct, 1), :][None])

        square, inner = lax.fori_loop(0, nct, moments, (zero, zero))
        inverse = lax.rsqrt(jnp.sum(square, axis=-1, keepdims=True) * inv_c + 1e-06)
        along = jnp.sum(inner, axis=-1, keepdims=True) * inv_c * inverse

        def finish(ct, r=r, newest=newest, center=center, inverse=inverse, scaled_mean=scaled_mean, along=along):
            upstream = n3[ct, r]
            normed = (mixed[ct, r] - center) * inverse
            scaled = upstream * gain[pl.ds(ct, 1), :][None]
            grad = inverse * (scaled - scaled_mean - normed * along)
            grad = grad.astype(BF16).astype(F32)
            for t, value in ((49, grad), (50, upstream * normed), (51, upstream)):
                part = jnp.sum(value, axis=0)
                if not newest:
                    part = part + pacc[ct, tap_rows(t), :]
                pacc[ct, tap_rows(t), :] = part
            for k in range(segw):
                tmp[6, pl.ds(8 + k, SEGS, stride=segw), :] = grad[k]
            g_own[r, :, lanes(ct)] = tmp[6, pl.ds(8, cols), :].astype(BF16)
            for k in range(wide):
                g3[ct, 3 + r, k] = tmp[6, pl.ds(8 - KERNEL // 2 + k, SEGS, stride=segw), :]

        loop(finish)

        @pl.when(has_cross)
        def _(r=r):
            gx[r].start()

        gs[r].start()

        def taps(ct, r=r, newest=newest):
            grad = g3[ct, 3 + r, pl.ds(KERNEL // 2, segw)]
            for a in range(KERNEL):
                line = f3[ct, r + a]
                for b in range(KERNEL):
                    row = pl.ds(pl.multiple_of((flip(a, KERNEL) * KERNEL + b) * 8, 8), 8)
                    part = jnp.sum(grad * line[b:b + segw], axis=0)
                    if not newest:
                        part = part + pacc[ct, row, :]
                    pacc[ct, row, :] = part

        loop(taps)

    def gather_taps(ct):
        pacc[ct, pl.ds(52 * 8, 32), :] = jnp.zeros((32, LANES), F32)
        for t in range(0, TAP_ROWS, 8):
            part = pacc[ct, pl.ds(t * 8, 8, stride=8), :]
            for i in range(1, 8):
                part = part + pacc[ct, pl.ds(t * 8 + i, 8, stride=8), :]
            pg[ct, pl.ds(t, 8), :] = part

    loop(gather_taps)

    used = pl.ds(0, TAP_ROWS)
    send_a = remote(pg.at[pl.ds(halfct * (1 - core), halfct), used], ra, a_s, a_r, sib)
    send_a.start()

    for r in range(rows):
        gs[r].wait_recv()
    both(*[widen(g_sib, r, g3, 8 - r, r) for r in range(rows)])

    def backward_near(ct):
        acc = conv(ct, [resid[ct, r] for r in range(rows)], g3, near, True)
        for r in range(rows):
            mixed[ct, r] = acc[r]

    def span(body, low, high):
        lax.fori_loop(low, high, lambda ct, c: (body(ct), c)[1], 0)

    span(backward_near, 0, nct // 3)
    send_a.wait_recv()

    def add_a(ct):
        pg[halfct * core + ct, used, :] += ra[ct]

    span(add_a, 0, halfct)

    third = halfct // nx
    sends_b = []
    for d in range(1, nx):
        to = lax.rem(x + d, nx)
        sends_b.append(remote(
            pg.at[pl.ds(halfct * core + third * to, third), used], rb.at[d - 1], b_s.at[d - 1], b_r.at[d - 1],
            dev(z, y, to, core),
        ))
    for copy in sends_b:
        copy.start()
    span(backward_near, nct // 3, nct)
    for copy in sends_b:
        copy.wait_recv()
    sb[...] = jnp.zeros_like(sb)
    for i in range(third):
        part = pg[halfct * core + third * x + i, used, :]
        for d in range(nx - 1):
            part = part + rb[d, i]
        sb[i, used, :] = part

    sends_c = []
    for d in range(1, ny):
        to = lax.rem(y + d, ny)
        sends_c.append(remote(
            sb.at[:, pl.ds(pl.multiple_of(per_y * to, per_y), per_y)], rc.at[d - 1], c_s.at[d - 1], c_r.at[d - 1],
            dev(z, to, x, core),
        ))
    for copy in sends_c:
        copy.start()
    for copy in sends_c:
        copy.wait_recv()
    part = sb[:, pl.ds(pl.multiple_of(per_y * y, per_y), per_y), :]
    for d in range(ny - 1):
        part = part + rc[d]
    sc[...] = part

    sends_d = []
    for j in range(2):
        to = 2 * m + j
        slot = lax.rem(z - to + nz - 1, nz)
        sends_d.append(remote(sc.at[pl.ds(j, 2)], rd.at[slot], d_s.at[j], d_r.at[slot], dev(to, y, x, core)))

        @pl.when(z != to)
        def _(j=j):
            sends_d[j].start()

    owner = lax.div(z, 2) == m
    others = lax.div(z, 2) != m
    sends_e = []
    for d in range(1, 2 * nx):
        flat = lax.rem(m + d, 2 * nx)
        sends_e.append(remote(sd, sd, e_s.at[d - 1], e_r, dev(z, y, lax.rem(flat, nx), lax.div(flat, nx))))

    @pl.when(owner)
    def _():
        for d in range(nz - 1):
            remote(sc.at[pl.ds(0, 2)], rd.at[d], d_s.at[0], d_r.at[d], sib).wait_recv()
        part = sc[pl.ds(lax.rem(z, 2), 2)]
        for d in range(nz - 1):
            part = part + rd[d]
        sd[...] = part
        for copy in sends_e:
            copy.start()

    @pl.when(others)
    def _():
        sends_e[0].wait_recv()

    mine = pl.ds(pl.multiple_of(per_y * y, per_y), per_y)
    sends_h = [
        remote(sd, pf.at[:, mine], h_s.at[d - 1], h_r.at[d - 1], dev(z, lax.rem(y + d, ny), x, core))
        for d in range(1, ny)
    ]
    for copy in sends_h:
        copy.start()
    pf[:, mine, :] = sd[...]

    for r in reversed(range(rows)):
        @pl.when(has_cross)
        def _(r=r):
            gx[2 - r].wait_recv()

    def backward_far(ct):
        for e in range(3):
            widen(g_cross, 2 - e, g3, e, e)(ct)
        acc = [mixed[ct, i] for i in range(rows)]
        acc = conv(ct, acc, g3, [(e, i) for e, i in all_combos if e < 3], True)
        for r in range(rows):
            for k in range(segw):
                tmp[3 + r, pl.ds(8 + k, SEGS, stride=segw), :] = acc[r][k]
            o_own[r, :, lanes(ct)] = tmp[3 + r, pl.ds(8, cols), :].astype(BF16)

    loop(backward_far)
    outs = [pltpu.make_async_copy(o_own.at[r], out_ig.at[0, flip(r, rows)], out_sem.at[r]) for r in range(rows)]
    for copy in outs:
        copy.start()
    for copy in sends_h:
        copy.wait_recv()
    out_pg[...] = pf[...]
    for copy in outs:
        copy.wait()

    for r in range(rows):
        fs[r].wait_send()
        gs[r].wait_send()

    @pl.when(has_cross)
    def _():
        for r in range(rows):
            fx[r].wait_send()
            gx[r].wait_send()

    @pl.when(s < 3)
    def _():
        t_next.wait_send()

    @pl.when(s > 0)
    def _():
        t_prev.wait_send()

    send_a.wait_send()
    for copy in sends_b + sends_c + sends_h:
        copy.wait_send()
    for j in range(2):
        @pl.when(z != 2 * m + j)
        def _(j=j):
            sends_d[j].wait_send()

    @pl.when(owner)
    def _():
        for copy in sends_e:
            copy.wait_send()


def body(features, norm_grad, token_grads, token_place, valid_rows, depth_kernel, depth_bias, norm_gain):
    rows, cols, channels = features.shape[1:]
    seq = token_grads.shape[1]
    nct = channels // LANES
    nx, ny_lo = NX, NY_LO
    dp_size = lax.axis_size("dp")
    nz = dp_size // (nx * ny_lo)
    ny = 2 * ny_lo
    per_y = 64 // ny
    segw = cols // SEGS
    wide = segw + KERNEL - 1
    third = nct // 2 // nx
    any_spec = pl.BlockSpec(memory_space=pl.ANY)
    vmem = pl.BlockSpec(memory_space=pltpu.VMEM)
    smem = pl.BlockSpec(memory_space=pltpu.SMEM)
    line = (rows, cols, channels)
    dma = pltpu.SemaphoreType.DMA
    tail = token_grads[0, seq - 32:]
    input_grads, sums = pl.pallas_call(
        functools.partial(fused, (nz, ny_lo, nx, nct, rows, cols, seq)),
        out_shape=(
            jax.ShapeDtypeStruct(features.shape, BF16),
            jax.ShapeDtypeStruct((2, 64, LANES), F32),
        ),
        in_specs=[any_spec] * 5 + [smem] * 2 + [vmem] * 2,
        out_specs=(any_spec, vmem),
        scratch_shapes=[
            pltpu.VMEM(line, BF16),
            pltpu.VMEM(line, BF16),
            pltpu.VMEM(line, BF16),
            pltpu.VMEM(line, BF16),
            pltpu.VMEM((240, channels), BF16),
            pltpu.VMEM(depth_kernel.shape, BF16),
            pltpu.VMEM(line, BF16),
            pltpu.VMEM(line, BF16),
            pltpu.VMEM(line, BF16),
            pltpu.VMEM(line, BF16),
            pltpu.VMEM((nct, rows + 6, wide, SEGS, LANES), F32),
            pltpu.VMEM((nct, rows + 6, wide, SEGS, LANES), F32),
            pltpu.VMEM((nct, rows, segw, SEGS, LANES), F32),
            pltpu.VMEM((nct, KERNEL * KERNEL * 8, LANES), F32),
            pltpu.VMEM((nct, rows, segw, SEGS, LANES), F32),
            pltpu.VMEM((nct, rows, segw, SEGS, LANES), F32),
            pltpu.VMEM((rows * cols, 240), F32),
            pltpu.VMEM((7, 64, LANES), F32),
            pltpu.VMEM((nct, TAP_ROWS * 8, LANES), F32),
            pltpu.VMEM((nct, TAP_ROWS, LANES), F32),
            pltpu.VMEM((nct // 2, TAP_ROWS, LANES), F32),
            pltpu.VMEM((max(nx - 1, 1), third, TAP_ROWS, LANES), F32),
            pltpu.VMEM((third, 64, LANES), F32),
            pltpu.VMEM((ny - 1, third, per_y, LANES), F32),
            pltpu.VMEM((third, per_y, LANES), F32),
            pltpu.VMEM((nz - 1, 2, per_y, LANES), F32),
            pltpu.VMEM((2, per_y, LANES), F32),
            pltpu.VMEM((2, 64, LANES), F32),
            dma((9,)), dma((rows,)),
            dma((rows,)), dma((rows,)), dma((rows,)), dma((rows,)),
            dma((rows,)), dma((rows,)), dma((rows,)), dma((rows,)),
            dma((2,)), dma((2,)),
            dma, dma,
            dma((max(nx - 1, 1),)), dma((max(nx - 1, 1),)),
            dma((ny - 1,)), dma((ny - 1,)),
            dma((2,)), dma((nz - 1,)),
            dma((2 * nx - 1,)), dma,
            dma((ny - 1,)), dma((ny - 1,)),
        ],
        compiler_params=pltpu.CompilerParams(
            collective_id=0, has_side_effects=True, vmem_limit_bytes=60 * 1024 * 1024,
        ),
    )(
        features, norm_grad, token_grads, tail, depth_kernel, token_place, valid_rows,
        depth_bias.reshape(nct, LANES), norm_gain.reshape(nct, LANES),
    )
    index = lax.axis_index("dp")
    count = channels // dp_size
    start = 64 * (index // (nx * ny_lo) % 2) + count * (index % (nx * ny_lo))
    wide_sums = jnp.concatenate([sums[0], sums[1]], axis=1)
    param_grads = lax.dynamic_slice(wide_sums, (0, start), (KERNEL * KERNEL + 3, count))
    return input_grads, param_grads


def solution(mesh):
    placed = (
        P("dp", "space", None, None),
        P("dp", "space", None, None),
        P("dp", "space", None),
        P("dp", "space", None),
        P("dp"),
        P(),
        P(),
        P(),
    )
    return jax.shard_map(
        body,
        mesh=mesh,
        in_specs=placed,
        out_specs=(P("dp", "space", None, None), P(None, "dp")),
        check_vma=False,
    )
```

time: 1880 us -> 107 us (0.06)
  starting transfers between devices: 1050 us -> 0 us
  blocking collectives: 700 us -> 0 us
  Pallas kernels: 0 us -> 98.5 us
  local copies, waits for them, and re-layouts: 57.4 us -> 5.85 us
  matrix products: 43.7 us -> 0 us
    unnamed x64 -> x0, starting transfers between devices: 1010 us -> none
    unnamed x1 -> x0, blocking collectives: 681 us -> none
    pallas_call x0 -> x1, Pallas kernels: none -> 98.5 us  [body(): pl.pallas_call(functools.partial(fused, (nz, ny_lo, nx, nct, rows, cols,...]
    conv_general_dilated x3 -> x0, matrix products: 43.7 us -> none  [grouped_conv(): lax.conv_general_dilated(lhs, rhs, (1, 1), ((0, 0), (col_pad, col_pad)),...]
    ppermute x6 -> x0, starting transfers between devices: 35.4 us -> none  [the longest x3 18.5 us: padded(): lax.ppermute(lax.slice_in_dim(block, block.shape[dim] - width, None, axis...]
    conv_general_dilated x10 -> x0, local copies, waits for them, and re-layouts: 20.6 us -> none  [grouped_conv(): lax.conv_general_dilated(lhs, rhs, (1, 1), ((0, 0), (col_pad, col_pad)),...]
  transfers between devices with their start and end apart: 70 -> 0, of which waited for: 2 -> 0; matrix products, arithmetic and copies ran while one was open for 41% -> 0% of each run, Pallas kernels for 0% -> 0%
where the time goes in v1:
time: 107 us; the launch traced here: 106 us
  Pallas kernels  98.5 us (92%)
  local copies, waits for them, and re-layouts  5.85 us (5%)
  between operations  1.35 us (1%)
    pallas_call x1, Pallas kernels, body(): pl.pallas_call(functools.partial(fused, (nz, ny_lo, nx, nct, rows, cols,...  98.5 us
    unnamed x5, local copies, waits for them, and re-layouts  3.4 us

profile of v1, /device:TPU:1, one launch (start us, length us, event | category | flops | bytes accessed | tf_op | source)
XLA Modules:
  0.0 105.7 jit_solution(5283189009146095156)
XLA Ops:
  0.7 0.0 copy-start
  0.7 1.7 %slice_bitcast_fusion.tail = bf16[32,3072]{1,0:T(8,128)(2,1)} fusion(bf16[1,155,3072]{2,1,0:T(8,128)(2,1)} %tok.1), kind=kLoop, calls=%fused_computation | loop fusion | bytes 393216 | tf_op jit(solution)/shard_map/squeeze | solution.py:500
  2.4 0.0 copy-done
  2.4 0.6 copy.10.place
  3.6 98.5 %shard_map.95 = (bf16[1,3,48,3072]{3,2,1,0:T(8,128)(2,1)}, f32[2,64,128]{2,1,0:T(8,128)}) custom-call(bf16[1,3,48,3072]{3,2,1,0:T(8,128)(2,1)} %feat.1, bf16[1,3,48,3072]{3,2,1,0:T(8,128)(2,1)} %ngrad.1, bf16[1,155,3072]{2,1,0:T(8,128)(2,1)} %tok.1, bf16[32,3072]{1,0:T(8,128)(2,1)} %slice_bitcast_fusion.tail, bf16[7,7,3072]{2,1,0:T(8,128)(2,1)} %dk.1, ...), custom_call_target="tpu_custom_call" | custom-call | tf_op jit(solution)/shard_map/pallas_call | solution.py:501
  102.1 0.8 slice_bitcast_fusion.1
  102.8 0.1 fusion
  102.9 0.7 copy.11
  103.6 2.1 %copy.14 = bf16[1,3,48,3072]{3,2,1,0:T(8,128)(2,1)} copy(bf16[1,3,48,3072]{3,2,1,0:T(8,128)(2,1)} %get-tuple-element.12) | data formatting | bytes 1769472
Async XLA Ops:
  0.7 1.7 %copy-start = (s32[1,3,48]{2,0,1:T(1,128)S(1)}, s32[1,3,48]{2,0,1:T(1,128)}, u32[]{:S(2)}) copy-start(s32[1,3,48]{2,0,1:T(1,128)} %param.11) | copy-start | bytes 1732

commit v2 on v1

--- a/solution.py
+++ b/solution.py
@@ -18,9 +18,9 @@
 
 
 def fused(
-    sizes, feat, ngrad, tok, tail, dk, place, valid, bias, gain, out_ig, out_pg,
-    f_own, f_sib, f_cross, n_own, t_all, k_raw, g_own, g_sib, g_cross, o_own,
-    f3, g3, n3, w8, mixed, resid, onehot, tmp, pacc, pg, ra, rb, sb, rc, sc, rd, sd, pf,
+    sizes, feat, ngrad, tok, dk, place, valid, bias, gain, out_ig, out_pg,
+    f_own, f_sib, f_cross, n_own, t_own, t_tail, t_side, p_own, k_raw, g_own, g_sib, g_cross, o_own,
+    f3, g3, n3, w8, mixed, resid, hot_own, hot_side, tmp, pacc, pg, ra, rb, sb, rc, sc, rd, sd, pf,
     local_sem, out_sem, fs_s, fs_r, fx_s, fx_r, gs_s, gs_r, gx_s, gx_r, t_s, t_r,
     a_s, a_r, b_s, b_r, c_s, c_r, d_s, d_r, e_s, e_r, h_s, h_r,
 ):
@@ -62,10 +62,12 @@
     for r in range(rows):
         local.append(pltpu.make_async_copy(feat.at[0, flip(r, rows)], f_own.at[r], local_sem.at[1 + r]))
         local.append(pltpu.make_async_copy(ngrad.at[0, flip(r, rows)], n_own.at[r], local_sem.at[4 + r]))
-    local.append(pltpu.make_async_copy(tok.at[0, pl.ds(0, 144)], t_all.at[pl.ds(32, 144)], local_sem.at[7]))
-    local.append(pltpu.make_async_copy(tail, t_all.at[pl.ds(176, 32)], local_sem.at[8]))
+    local.append(pltpu.make_async_copy(tok.at[0], t_own, local_sem.at[7]))
+    local.append(pltpu.make_async_copy(place, p_own, local_sem.at[8]))
     for copy in local:
         copy.start()
+
+    t_side[...] = jnp.zeros_like(t_side)
 
     barrier = pltpu.get_barrier_semaphore()
 
@@ -86,48 +88,6 @@
         greet(dev(lax.rem(z + d, nz), y, x, core))
     peers = 2 * nx - 1 + ny - 1 + nz - 1
 
-    @pl.when(has_cross)
-    def _():
-        pl.semaphore_wait(barrier, peers + 1)
-
-    @pl.when(no_cross)
-    def _():
-        pl.semaphore_wait(barrier, peers)
-
-    fx = [remote(feat.at[0, flip(r, rows)], f_cross.at[r], fx_s.at[r], fx_r.at[r], cross) for r in range(rows)]
-    fs = [remote(feat.at[0, flip(r, rows)], f_sib.at[r], fs_s.at[r], fs_r.at[r], sib) for r in range(rows)]
-    t_next = remote(tail, t_all.at[pl.ds(0, 32)], t_s.at[0], t_r.at[0], (dp, s + 1))
-    t_prev = remote(tok.at[0, pl.ds(0, 32)], t_all.at[pl.ds(208, 32)], t_s.at[1], t_r.at[1], (dp, s - 1))
-
-    @pl.when(has_cross)
-    def _():
-        for r in range(rows):
-            fx[r].start()
-
-    for r in range(rows):
-        fs[r].start()
-
-    @pl.when(s < 3)
-    def _():
-        t_next.start()
-
-    @pl.when(s > 0)
-    def _():
-        t_prev.start()
-
-    @pl.when(no_cross)
-    def _():
-        f_cross[...] = jnp.zeros_like(f_cross)
-        g_cross[...] = jnp.zeros_like(g_cross)
-
-    @pl.when(s == 0)
-    def _():
-        t_all[pl.ds(0, 32), :] = jnp.zeros((32, channels), BF16)
-
-    @pl.when(s == 3)
-    def _():
-        t_all[pl.ds(208, 32), :] = jnp.zeros((32, channels), BF16)
-
     tmp[...] = jnp.zeros_like(tmp)
 
     def lanes(ct):
@@ -147,6 +107,35 @@
 
     loop(spread)
 
+    @pl.when(has_cross)
+    def _():
+        pl.semaphore_wait(barrier, peers + 1)
+
+    @pl.when(no_cross)
+    def _():
+        pl.semaphore_wait(barrier, peers)
+
+    fx = [remote(feat.at[0, flip(r, rows)], f_cross.at[r], fx_s.at[r], fx_r.at[r], cross) for r in range(rows)]
+    fs = [remote(feat.at[0, flip(r, rows)], f_sib.at[r], fs_s.at[r], fs_r.at[r], sib) for r in range(rows)]
+    t_next = remote(t_tail, t_side.at[pl.ds(0, 32)], t_s.at[0], t_r.at[0], sib)
+    t_prev = remote(tok.at[0, pl.ds(0, 32)], t_side.at[pl.ds(32, 32)], t_s.at[0], t_r.at[0], sib)
+    t_next_x = remote(t_tail.at[pl.ds(16, 16)], t_side.at[pl.ds(16, 16)], t_s.at[1], t_r.at[1], cross)
+    t_prev_x = remote(tok.at[0, pl.ds(0, 16)], t_side.at[pl.ds(32, 16)], t_s.at[1], t_r.at[1], cross)
+
+    def send_row(r):
+        @pl.when(has_cross)
+        def _():
+            fx[r].start()
+
+    send_row(0)
+    for r in range(rows):
+        fs[r].start()
+
+    @pl.when(no_cross)
+    def _():
+        f_cross[...] = jnp.zeros_like(f_cross)
+        g_cross[...] = jnp.zeros_like(g_cross)
+
     def weight(ct, a, b):
         return w8[ct, pl.ds((a * KERNEL + b) * 8, 8), :][None]
 
@@ -173,6 +162,7 @@
                 n3[ct, r, k] = tmp[3 + r, pl.ds(8 + k, SEGS, stride=segw), :]
 
     both(*[widen(f_own, r, f3, 3 + r, r) for r in range(rows)], stage_grad)
+    send_row(1)
     for r in range(rows):
         fs[r].wait_recv()
     both(*[widen(f_sib, r, f3, 8 - r, r) for r in range(rows)])
@@ -200,38 +190,71 @@
             mixed[ct, r] = acc[r]
 
     loop(forward_near)
+    send_row(2)
 
     local[7].wait()
     local[8].wait()
-
-    @pl.when(s > 0)
-    def _():
+    where_tail = lax.broadcasted_iota(jnp.int32, (32, seq), 1) - lax.broadcasted_iota(jnp.int32, (32, seq), 0)
+    tail_rows = jnp.where(where_tail == seq - 32, 1.0, 0.0).astype(BF16)
+
+    group = 6
+
+    def broad(i):
+        return pl.ds(pl.multiple_of(i * group * LANES, group * LANES), group * LANES)
+
+    def cut_tail(i, carry):
+        found = jnp.dot(tail_rows, t_own[:, broad(i)], preferred_element_type=F32)
+        t_tail[:, broad(i)] = found.astype(BF16)
+        return carry
+
+    lax.fori_loop(0, nct // group, cut_tail, 0)
+
+    @pl.when(core == 0)
+    def _():
+        t_next.start()
+
+    @pl.when(core == 1)
+    def _():
+        t_prev.start()
+
+    @pl.when(s == 1)
+    def _():
+        t_next_x.start()
+
+    @pl.when(s == 2)
+    def _():
+        t_prev_x.start()
+
+    def pick_tokens():
         t_next.wait_recv()
 
-    @pl.when(s < 3)
-    def _():
-        t_prev.wait_recv()
-
-    first = place[0, 0, 0] - s * seq
-    held = valid[0] - s * rows
-    width = t_all.shape[0]
-    lane = lax.broadcasted_iota(jnp.int32, (SEGS, width), 1)
-    seg = lax.broadcasted_iota(jnp.int32, (SEGS, width), 0)
-    late = jnp.where(lane < 208, lane - 176 + (seq - 32), lane - 208 + seq)
-    late = jnp.where(late < 144, -4096, late)
-    position = jnp.where(lane < 176, lane - 32, late)
-    for r in range(rows):
-        row = flip(r, rows)
-        base = jnp.where(row < held, first + row * (cols + 1), -8192)
-        for k in range(segw):
-            hit = position == base + segw * seg + k
-            onehot[pl.ds((r * segw + k) * SEGS, SEGS), :] = jnp.where(hit, 1.0, 0.0).astype(F32)
-
-    def pick(ct):
-        found = jnp.dot(onehot[...].astype(BF16), t_all[:, lanes(ct)], preferred_element_type=F32)
-        resid[ct] = found.reshape(rows, segw, SEGS, LANES)
-
-    loop(pick)
+        @pl.when(has_cross)
+        def _():
+            t_next_x.wait_recv()
+
+        first = p_own[0, pl.ds(0, 1), pl.ds(0, 1)] - s * seq
+        held = valid[0] - s * rows
+        for r in range(rows):
+            row = flip(r, rows)
+            base = first + jnp.where(row < held, row * (cols + 1), -8192)
+            for k in range(segw):
+                target = base + k + segw * lax.broadcasted_iota(jnp.int32, (SEGS, 1), 0)
+                at = pl.ds((r * segw + k) * SEGS, SEGS)
+                lane = lax.broadcasted_iota(jnp.int32, (SEGS, seq), 1)
+                hot_own[at, :] = jnp.where(lane == target, 1.0, 0.0).astype(F32)
+                lane = lax.broadcasted_iota(jnp.int32, (SEGS, 64), 1)
+                lane = jnp.where(lane < 32, lane - 32, lane - 32 + seq)
+                hot_side[at, :] = jnp.where(lane == target, 1.0, 0.0).astype(F32)
+
+        def pick(i, carry):
+            found = jnp.dot(hot_own[...].astype(BF16), t_own[:, broad(i)], preferred_element_type=F32)
+            found += jnp.dot(hot_side[...].astype(BF16), t_side[:, broad(i)], preferred_element_type=F32)
+            for j in range(group):
+                part = found[:, j * LANES:(j + 1) * LANES]
+                resid[i * group + j] = part.reshape(rows, segw, SEGS, LANES)
+            return carry
+
+        lax.fori_loop(0, nct // group, pick, 0)
 
     inv_c = 1.0 / channels
     gx = [remote(g_own.at[r], g_cross.at[r], gx_s.at[r], gx_r.at[r], cross) for r in range(rows)]
@@ -293,9 +316,10 @@
 
         loop(finish)
 
-        @pl.when(has_cross)
-        def _(r=r):
-            gx[r].start()
+        if r > 0:
+            @pl.when(has_cross)
+            def _(r=r):
+                gx[r].start()
 
         gs[r].start()
 
@@ -310,7 +334,8 @@
                         part = part + pacc[ct, row, :]
                     pacc[ct, row, :] = part
 
-        loop(taps)
+        if r > 0:
+            loop(taps)
 
     def gather_taps(ct):
         pacc[ct, pl.ds(52 * 8, 32), :] = jnp.zeros((32, LANES), F32)
@@ -320,43 +345,56 @@
                 part = part + pacc[ct, pl.ds(t * 8 + i, 8, stride=8), :]
             pg[ct, pl.ds(t, 8), :] = part
 
-    loop(gather_taps)
-
     used = pl.ds(0, TAP_ROWS)
-    send_a = remote(pg.at[pl.ds(halfct * (1 - core), halfct), used], ra, a_s, a_r, sib)
-    send_a.start()
+    third = halfct // nx
+    sends_a, sends_b = [], []
+    for d in range(nx):
+        to = lax.rem(x + 1 + d, nx)
+        away = halfct * (1 - core) + third * to
+        mine = halfct * core + third * to
+        sends_a.append(remote(pg.at[pl.ds(away, third), used], ra.at[d], a_s.at[d], a_r.at[d], sib))
+        if d < nx - 1:
+            sends_b.append(remote(
+                pg.at[pl.ds(mine, third), used], rb.at[d], b_s.at[d], b_r.at[d], dev(z, y, to, core),
+            ))
+
+    def span(body, low, high):
+        lax.fori_loop(low, high, lambda ct, c: (body(ct), c)[1], 0)
+
+    def pass_on(d):
+        sends_a[d].wait_recv()
+        mine = halfct * core + third * lax.rem(x + 1 + d, nx)
+        for i in range(third):
+            pg[mine + i, used, :] += ra[d, i]
+        if d < nx - 1:
+            sends_b[d].start()
+
+    for d in range(nx):
+        to = third * lax.rem(x + 1 + d, nx)
+
+        def last_taps(i, to=to):
+            other = jnp.where(i < third, 1 - core, core)
+            ct = halfct * other + to + lax.rem(i, third)
+            taps(ct)
+            gather_taps(ct)
+
+        span(last_taps, 0, 2 * third)
+        sends_a[d].start()
+        if d > 0:
+            pass_on(d - 1)
+    pass_on(nx - 1)
 
     for r in range(rows):
         gs[r].wait_recv()
     both(*[widen(g_sib, r, g3, 8 - r, r) for r in range(rows)])
 
     def backward_near(ct):
-        acc = conv(ct, [resid[ct, r] for r in range(rows)], g3, near, True)
+        zero = jnp.zeros((segw, SEGS, LANES), F32)
+        acc = conv(ct, [zero] * rows, g3, near, True)
         for r in range(rows):
             mixed[ct, r] = acc[r]
 
-    def span(body, low, high):
-        lax.fori_loop(low, high, lambda ct, c: (body(ct), c)[1], 0)
-
-    span(backward_near, 0, nct // 3)
-    send_a.wait_recv()
-
-    def add_a(ct):
-        pg[halfct * core + ct, used, :] += ra[ct]
-
-    span(add_a, 0, halfct)
-
-    third = halfct // nx
-    sends_b = []
-    for d in range(1, nx):
-        to = lax.rem(x + d, nx)
-        sends_b.append(remote(
-            pg.at[pl.ds(halfct * core + third * to, third), used], rb.at[d - 1], b_s.at[d - 1], b_r.at[d - 1],
-            dev(z, y, to, core),
-        ))
-    for copy in sends_b:
-        copy.start()
-    span(backward_near, nct // 3, nct)
+    span(backward_near, 0, nct // 4)
     for copy in sends_b:
         copy.wait_recv()
     sb[...] = jnp.zeros_like(sb)
@@ -375,6 +413,12 @@
         ))
     for copy in sends_c:
         copy.start()
+
+    @pl.when(has_cross)
+    def _():
+        gx[0].start()
+
+    span(backward_near, nct // 4, nct // 2)
     for copy in sends_c:
         copy.wait_recv()
     part = sb[:, pl.ds(pl.multiple_of(per_y * y, per_y), per_y), :]
@@ -392,6 +436,7 @@
         def _(j=j):
             sends_d[j].start()
 
+    span(backward_near, nct // 2, 3 * nct // 4)
     owner = lax.div(z, 2) == m
     others = lax.div(z, 2) != m
     sends_e = []
@@ -399,6 +444,12 @@
         flat = lax.rem(m + d, 2 * nx)
         sends_e.append(remote(sd, sd, e_s.at[d - 1], e_r, dev(z, y, lax.rem(flat, nx), lax.div(flat, nx))))
 
+    mine = pl.ds(pl.multiple_of(per_y * y, per_y), per_y)
+    sends_h = [
+        remote(sd, pf.at[:, mine], h_s.at[d - 1], h_r.at[d - 1], dev(z, lax.rem(y + d, ny), x, core))
+        for d in range(1, ny)
+    ]
+
     @pl.when(owner)
     def _():
         for d in range(nz - 1):
@@ -407,20 +458,18 @@
         for d in range(nz - 1):
             part = part + rd[d]
         sd[...] = part
-        for copy in sends_e:
+        for copy in sends_e + sends_h:
             copy.start()
 
+    span(backward_near, 3 * nct // 4, nct)
+    pick_tokens()
+
     @pl.when(others)
     def _():
         sends_e[0].wait_recv()
-
-    mine = pl.ds(pl.multiple_of(per_y * y, per_y), per_y)
-    sends_h = [
-        remote(sd, pf.at[:, mine], h_s.at[d - 1], h_r.at[d - 1], dev(z, lax.rem(y + d, ny), x, core))
-        for d in range(1, ny)
-    ]
-    for copy in sends_h:
-        copy.start()
+        for copy in sends_h:
+            copy.start()
+
     pf[:, mine, :] = sd[...]
 
     for r in reversed(range(rows)):
@@ -431,7 +480,7 @@
     def backward_far(ct):
         for e in range(3):
             widen(g_cross, 2 - e, g3, e, e)(ct)
-        acc = [mixed[ct, i] for i in range(rows)]
+        acc = [mixed[ct, i] + resid[ct, i] for i in range(rows)]
         acc = conv(ct, acc, g3, [(e, i) for e, i in all_combos if e < 3], True)
         for r in range(rows):
             for k in range(segw):
@@ -444,7 +493,8 @@
         copy.start()
     for copy in sends_h:
         copy.wait_recv()
-    out_pg[...] = pf[...]
+    out_pg[:, pl.ds(0, LANES)] = pf[0]
+    out_pg[:, pl.ds(LANES, LANES)] = pf[1]
     for copy in outs:
         copy.wait()
 
@@ -458,16 +508,23 @@
             fx[r].wait_send()
             gx[r].wait_send()
 
-    @pl.when(s < 3)
+    @pl.when(core == 0)
     def _():
         t_next.wait_send()
 
-    @pl.when(s > 0)
+    @pl.when(core == 1)
     def _():
         t_prev.wait_send()
 
-    send_a.wait_send()
-    for copy in sends_b + sends_c + sends_h:
+    @pl.when(s == 1)
+    def _():
+        t_next_x.wait_send()
+
+    @pl.when(s == 2)
+    def _():
+        t_prev_x.wait_send()
+
+    for copy in sends_a + sends_b + sends_c + sends_h:
         copy.wait_send()
     for j in range(2):
         @pl.when(z != 2 * m + j)
@@ -497,21 +554,23 @@
     smem = pl.BlockSpec(memory_space=pltpu.SMEM)
     line = (rows, cols, channels)
     dma = pltpu.SemaphoreType.DMA
-    tail = token_grads[0, seq - 32:]
     input_grads, sums = pl.pallas_call(
         functools.partial(fused, (nz, ny_lo, nx, nct, rows, cols, seq)),
         out_shape=(
             jax.ShapeDtypeStruct(features.shape, BF16),
-            jax.ShapeDtypeStruct((2, 64, LANES), F32),
+            jax.ShapeDtypeStruct((64, 2 * LANES), F32),
         ),
-        in_specs=[any_spec] * 5 + [smem] * 2 + [vmem] * 2,
+        in_specs=[any_spec] * 5 + [smem] + [vmem] * 2,
         out_specs=(any_spec, vmem),
         scratch_shapes=[
             pltpu.VMEM(line, BF16),
             pltpu.VMEM(line, BF16),
             pltpu.VMEM(line, BF16),
             pltpu.VMEM(line, BF16),
-            pltpu.VMEM((240, channels), BF16),
+            pltpu.VMEM((seq, channels), BF16),
+            pltpu.VMEM((32, channels), BF16),
+            pltpu.VMEM((64, channels), BF16),
+            pltpu.VMEM((rows, 1, cols), jnp.int32),
             pltpu.VMEM(depth_kernel.shape, BF16),
             pltpu.VMEM(line, BF16),
             pltpu.VMEM(line, BF16),
@@ -523,11 +582,12 @@
             pltpu.VMEM((nct, KERNEL * KERNEL * 8, LANES), F32),
             pltpu.VMEM((nct, rows, segw, SEGS, LANES), F32),
             pltpu.VMEM((nct, rows, segw, SEGS, LANES), F32),
-            pltpu.VMEM((rows * cols, 240), F32),
+            pltpu.VMEM((rows * cols, seq), F32),
+            pltpu.VMEM((rows * cols, 64), F32),
             pltpu.VMEM((7, 64, LANES), F32),
-            pltpu.VMEM((nct, TAP_ROWS * 8, LANES), F32),
+            pltpu.VMEM((nct, TAP_ROWS * 8 + 64, LANES), F32),
             pltpu.VMEM((nct, TAP_ROWS, LANES), F32),
-            pltpu.VMEM((nct // 2, TAP_ROWS, LANES), F32),
+            pltpu.VMEM((nx, third, TAP_ROWS, LANES), F32),
             pltpu.VMEM((max(nx - 1, 1), third, TAP_ROWS, LANES), F32),
             pltpu.VMEM((third, 64, LANES), F32),
             pltpu.VMEM((ny - 1, third, per_y, LANES), F32),
@@ -539,7 +599,7 @@
             dma((rows,)), dma((rows,)), dma((rows,)), dma((rows,)),
             dma((rows,)), dma((rows,)), dma((rows,)), dma((rows,)),
             dma((2,)), dma((2,)),
-            dma, dma,
+            dma((nx,)), dma((nx,)),
             dma((max(nx - 1, 1),)), dma((max(nx - 1, 1),)),
             dma((ny - 1,)), dma((ny - 1,)),
             dma((2,)), dma((nz - 1,)),
@@ -550,14 +610,13 @@
             collective_id=0, has_side_effects=True, vmem_limit_bytes=60 * 1024 * 1024,
         ),
     )(
-        features, norm_grad, token_grads, tail, depth_kernel, token_place, valid_rows,
+        features, norm_grad, token_grads, depth_kernel, jnp.transpose(token_place, (1, 0, 2)), valid_rows,
         depth_bias.reshape(nct, LANES), norm_gain.reshape(nct, LANES),
     )
     index = lax.axis_index("dp")
     count = channels // dp_size
     start = 64 * (index // (nx * ny_lo) % 2) + count * (index % (nx * ny_lo))
-    wide_sums = jnp.concatenate([sums[0], sums[1]], axis=1)
-    param_grads = lax.dynamic_slice(wide_sums, (0, start), (KERNEL * KERNEL + 3, count))
+    param_grads = lax.dynamic_slice(sums, (0, start), (KERNEL * KERNEL + 3, count))
     return input_grads, param_grads
 
 

time: 107 us -> 90.2 us (0.84)
  Pallas kernels: 98.5 us -> 84 us
  local copies, waits for them, and re-layouts: 5.85 us -> 3.72 us
    pallas_call x1, Pallas kernels: 98.5 us -> 84 us  [body(): pl.pallas_call(functools.partial(fused, (nz, ny_lo, nx, nct, rows, cols,...]
    squeeze x2 -> x0, local copies, waits for them, and re-layouts: 2.46 us -> none  [the longest x1 1.68 us: body(): tail = token_grads[0, seq - 32:]]
    unnamed x5 -> x2, local copies, waits for them, and re-layouts: 3.4 us -> 2.82 us
where the time goes in v2:
time: 90.2 us; the launch traced here: 89 us
  Pallas kernels  84 us (93%)
  local copies, waits for them, and re-layouts  3.72 us (4%)
  between operations  1.33 us (1%)
    pallas_call x1, Pallas kernels, body(): pl.pallas_call(functools.partial(fused, (nz, ny_lo, nx, nct, rows, cols,...  84 us
    unnamed x2, local copies, waits for them, and re-layouts  2.82 us

profile of v2, /device:TPU:1, one launch (start us, length us, event | category | flops | bytes accessed | tf_op | source)
XLA Modules:
  0.0 89.0 jit_solution(16036737702924103604)
XLA Ops:
  1.3 84.0 %shard_map.95 = (bf16[1,3,48,3072]{3,2,1,0:T(8,128)(2,1)}, f32[64,256]{1,0:T(8,128)}) custom-call(bf16[1,3,48,3072]{3,2,1,0:T(8,128)(2,1)} %feat.1, bf16[1,3,48,3072]{3,2,1,0:T(8,128)(2,1)} %ngrad.1, bf16[1,155,3072]{2,1,0:T(8,128)(2,1)} %tok.1, bf16[7,7,3072]{2,1,0:T(8,128)(2,1)} %dk.1, s32[3,1,48]{2,1,0:T(1,128)} %bitcast.5, s32[1]{0:T(128)S(6)} %copy.12.valid, ...), custom_call_target="tpu_custom_call" | custom-call | tf_op jit(solution)/shard_map/pallas_call | solution.py:557
  85.3 0.9 %constant_dynamic-slice_fusion = f32[52,12]{1,0:T(8,128)S(1)} fusion(f32[64,256]{1,0:T(8,128)} %get-tuple-element.5, s32[]{:T(128)S(6)} %select_n.21), kind=kLoop, calls=%fused_computation | loop fusion | bytes 4996 | tf_op jit(solution)/shard_map/dynamic_slice | solution.py:619
  86.2 0.7 copy.10
  86.9 2.1 %copy.13 = bf16[1,3,48,3072]{3,2,1,0:T(8,128)(2,1)} copy(bf16[1,3,48,3072]{3,2,1,0:T(8,128)(2,1)} %get-tuple-element.10) | data formatting | bytes 1769472
